TPU v7x, 32 devices: a whole 2x2x4 slice. The times are simulated.
32 devices in a mesh: rows: 4 (over z), seq: 8 (over y, x, core).
Axes of the slice: x: 2, y: 2, z: 4, core: 2. Of those that a mesh axis runs over, the one named last changes fastest.
Arguments:
- tokens: bfloat16 [8, 2048, 1024], P('rows', 'seq'), may hold values from -6 to 6
- cotangent: bfloat16 [8, 2048, 1024], P('rows', 'seq'), may hold values from -6 to 6
- bounds: int32 [8, 2], P('rows'), may hold values from 1 to 2048, as said below
- ln1_gain: bfloat16 [1024], replicated, may hold values from 0.5 to 1.5
- ln1_bias: bfloat16 [1024], replicated, may hold values from -1.25 to 1.25
- in_weight: bfloat16 [1024, 3072], replicated, may hold values from -0.1875 to 0.1875
- in_bias: bfloat16 [3072], replicated, may hold values from -1.75 to 1.75
- short_weight: bfloat16 [3, 3072], replicated, may hold values from -3.5 to 3.5
- short_bias: bfloat16 [3072], replicated, may hold values from -1.75 to 1.75
- f1_weight: bfloat16 [33, 64], replicated, may hold values from -6 to 6
- f1_bias: bfloat16 [64], replicated, may hold values from -6 to 6
- f2_weight: bfloat16 [64, 64], replicated, may hold values from -0.75 to 0.75
- f2_bias: bfloat16 [64], replicated, may hold values from -3 to 3
- f3_weight: bfloat16 [64, 1024], P(None, 'seq'), may hold values from -0.09375 to 0.09375
- filter_skip: bfloat16 [1024], P('seq'), may hold values from -6 to 6
- out_weight: bfloat16 [1024, 1024], replicated, may hold values from -0.1875 to 0.1875
- out_bias: bfloat16 [1024], replicated, may hold values from -1.25 to 1.25
- ln2_gain: bfloat16 [1024], replicated, may hold values from 0.5 to 1.5
- ln2_bias: bfloat16 [1024], replicated, may hold values from -1.25 to 1.25
- up_weight: bfloat16 [1024, 4096], replicated, may hold values from -0.1875 to 0.1875
- up_bias: bfloat16 [4096], replicated, may hold values from -1.75 to 1.75
- down_weight: bfloat16 [4096, 1024], replicated, may hold values from -0.09375 to 0.09375
- down_bias: bfloat16 [1024], replicated, may hold values from -1.25 to 1.25
Outputs:
- output: bfloat16 [8, 2048, 1024], P('rows', 'seq')
- grad_tokens: float32 [8, 2048, 1024], P('rows', 'seq')
- grad_ln1_gain: float32 [1024], P(('rows', 'seq'))
- grad_ln1_bias: float32 [1024], P(('rows', 'seq'))
- grad_in_weight: float32 [1024, 3072], P(('rows', 'seq'))
- grad_in_bias: float32 [3072], P(('rows', 'seq'))
- grad_short_weight: float32 [3, 3072], P(None, ('rows', 'seq'))
- grad_short_bias: float32 [3072], P(('rows', 'seq'))
- grad_f1_weight: float32 [33, 64], replicated
- grad_f1_bias: float32 [64], replicated
- grad_f2_weight: float32 [64, 64], replicated
- grad_f2_bias: float32 [64], replicated
- grad_f3_weight: float32 [64, 1024], P(None, 'seq')
- grad_filter_skip: float32 [1024], P('seq')
- grad_out_weight: float32 [1024, 1024], P(('rows', 'seq'))
- grad_out_bias: float32 [1024], P(('rows', 'seq'))
- grad_ln2_gain: float32 [1024], P(('rows', 'seq'))
- grad_ln2_bias: float32 [1024], P(('rows', 'seq'))
- grad_up_weight: float32 [1024, 4096], P(('rows', 'seq'))
- grad_up_bias: float32 [4096], P(('rows', 'seq'))
- grad_down_weight: float32 [4096, 1024], P(('rows', 'seq'))
- grad_down_bias: float32 [1024], P(('rows', 'seq'))
Inputs may be any that keep to these rules, and one draw needn't show every extreme that they name: `bounds`: in each row the cut points do not fall; a cut at 2048 starts no document; in every group of 2 rows on one index of rows one row is a single document.
All inputs are finite; a program needn't handle non-finite values.
Results may differ from a plain program's by a relative error of at most 0.0097.
Values may be sent and summed in bfloat16 or wider, within the bound.
No kernel may reach another device: no remote copies, remote signals or barrier semaphores. Data moves between devices by JAX's collectives and lax.ppermute only.
A program may use at most 384 MiB of HBM per device.

v0:
```python
import math

import jax
import jax.numpy as jnp
from jax import lax
from jax.sharding import PartitionSpec as P

D = 1024
EMB = 33


HIGH = lax.Precision.HIGHEST
eps = 1e-05
slow_rate = math.log(100.0) / 1.5
fast_rate = math.log(100.0) / 0.3


def passed_along(value, axis, steps):
    count = lax.axis_size(axis)
    first, last = (max(0, -steps), min(count, count - steps))
    return lax.ppermute(value, axis, [(source, source + steps) for source in range(first, last)])


def layer_norm(values, gain, shift):
    center = values - jnp.mean(values, axis=-1, keepdims=True)
    spread = jnp.mean(center * center, axis=-1, keepdims=True)
    return center * lax.rsqrt(spread + eps) * gain + shift


def gelu_tanh(values):
    return jax.nn.gelu(values, approximate=True)


def features(length):
    steps = jnp.arange(length, dtype=jnp.int32).astype(jnp.float32)
    bands = (EMB - 1) // 2
    freqs = 0.0001 + jnp.arange(bands, dtype=jnp.int32).astype(jnp.float32) * (
        (bands - 1 - 0.0001) / (bands - 1)
    )
    angles = (steps * (2.0 * math.pi / length))[:, None] * freqs[None, :]
    timeline = steps / (length - 1)
    return (
        jnp.concatenate([timeline[:, None], jnp.cos(angles), -jnp.sin(angles)], axis=1),
        timeline,
    )


def filter_taps(w_one, b_one, w_two, b_two, w_three, first, length):
    feats, timeline = features(length)
    hidden = jnp.sin(jnp.dot(feats, w_one, precision=HIGH) + b_one)
    hidden = jnp.sin(jnp.dot(hidden, w_two, precision=HIGH) + b_two)
    raw_taps = jnp.dot(hidden, w_three, precision=HIGH)
    channels = (first + jnp.arange(w_three.shape[1], dtype=jnp.int32)).astype(jnp.float32)
    rates = slow_rate + channels * ((fast_rate - slow_rate) / (D - 1))
    return raw_taps * jnp.exp(-timeline[:, None] * rates[None, :])


def document_masks(bounds, positions, length):
    lower = jnp.concatenate([jnp.zeros_like(bounds[:, :1]), bounds], axis=1)
    upper = jnp.concatenate([bounds, jnp.full_like(bounds[:, :1], length)], axis=1)
    inside = (positions[None, None, :] >= lower[:, :, None]) & (
        positions[None, None, :] < upper[:, :, None]
    )
    return inside.astype(jnp.float32)


def cos_sin(count_a, count_b, modulus):
    table = (
        jnp.arange(count_a, dtype=jnp.int32)[:, None]
        * jnp.arange(count_b, dtype=jnp.int32)[None, :]
        % modulus
    )
    angles = table.astype(jnp.float32) * (2.0 * math.pi / modulus)
    return (jnp.cos(angles), jnp.sin(angles))


def make_plan(blocks, block_len):
    outer = 2 * blocks
    cos_outer, sin_outer = cos_sin(outer, outer, outer)
    cos_twist, sin_twist = cos_sin(outer, block_len, outer * block_len)
    cos_inner, sin_inner = cos_sin(block_len, block_len, block_len)
    return (blocks, block_len, cos_outer, sin_outer, cos_twist, sin_twist, cos_inner, sin_inner)


def right_mul(left, table):
    return jnp.einsum("...km,mj->...kj", left, table, precision=HIGH)


def spectrum(series, plan):
    blocks, block_len, cos_outer, sin_outer, cos_twist, sin_twist, cos_inner, sin_inner = plan
    folded = series.reshape(series.shape[:-1] + (blocks, block_len))
    real_a = jnp.einsum("kn,...nm->...km", cos_outer[:, :blocks], folded, precision=HIGH)
    imag_a = -jnp.einsum("kn,...nm->...km", sin_outer[:, :blocks], folded, precision=HIGH)
    real_t = real_a * cos_twist + imag_a * sin_twist
    imag_t = imag_a * cos_twist - real_a * sin_twist
    real_x = right_mul(real_t, cos_inner) + right_mul(imag_t, sin_inner)
    imag_x = right_mul(imag_t, cos_inner) - right_mul(real_t, sin_inner)
    return (real_x, imag_x)


def inverse(real_x, imag_x, plan):
    blocks, block_len, cos_outer, sin_outer, cos_twist, sin_twist, cos_inner, sin_inner = plan
    real_b = right_mul(real_x, cos_inner) - right_mul(imag_x, sin_inner)
    imag_b = right_mul(imag_x, cos_inner) + right_mul(real_x, sin_inner)
    real_u = real_b * cos_twist - imag_b * sin_twist
    imag_u = imag_b * cos_twist + real_b * sin_twist
    folded = jnp.einsum("nk,...km->...nm", cos_outer[:blocks], real_u, precision=HIGH) - jnp.einsum(
        "nk,...km->...nm", sin_outer[:blocks], imag_u, precision=HIGH
    )
    folded = folded * (1.0 / (2 * blocks * block_len))
    return folded.reshape(folded.shape[:-2] + (blocks * block_len,))


def left_product(first_low, second_low):
    return jnp.einsum("ti,tj->ij", first_low, second_low, preferred_element_type=jnp.float32)


def back_product(grad_low, weight):
    return jnp.einsum("tj,ij->ti", grad_low, weight, preferred_element_type=jnp.float32)


def per_device(
    tokens,
    cotangent,
    bounds,
    ln1_gain,
    ln1_bias,
    in_weight,
    in_bias,
    short_weight,
    short_bias,
    f1_weight,
    f1_bias,
    f2_weight,
    f2_bias,
    f3_weight,
    filter_skip,
    out_weight,
    out_bias,
    ln2_gain,
    ln2_bias,
    up_weight,
    up_bias,
    down_weight,
    down_bias,
):
    seq_count = lax.axis_size("seq")
    row_count, tok_count, width = tokens.shape
    flat_count = row_count * tok_count
    length = tok_count * seq_count
    first_channel = lax.axis_index("seq") * f3_weight.shape[1]
    x_in = tokens.astype(jnp.float32).reshape(flat_count, width)
    n1, ln1_pull = jax.vjp(
        layer_norm, x_in, ln1_gain.astype(jnp.float32), ln1_bias.astype(jnp.float32)
    )
    n1_low = n1.astype(jnp.bfloat16)
    proj = jnp.dot(n1_low, in_weight, preferred_element_type=jnp.float32) + in_bias.astype(
        jnp.float32
    )
    proj_low = proj.astype(jnp.bfloat16).reshape(row_count, tok_count, 3 * width)
    here = lax.axis_index("seq") * tok_count + jnp.arange(tok_count, dtype=jnp.int32)
    starts = jnp.max(
        jnp.where(bounds[:, :, None] <= here[None, None, :], bounds[:, :, None], 0), axis=1
    )
    keep_one = (here[None, :] - 1 >= starts).astype(jnp.float32)[:, :, None]
    keep_two = (here[None, :] - 2 >= starts).astype(jnp.float32)[:, :, None]
    rim = passed_along(proj_low[:, tok_count - 2 :, :], "seq", 1)
    extended = jnp.concatenate([rim, proj_low], axis=1).astype(jnp.float32)
    current = extended[:, 2:, :]
    before_one = extended[:, 1:-1, :]
    before_two = extended[:, :-2, :]
    taps_short = short_weight.astype(jnp.float32)
    shorted = (
        taps_short[0] * current
        + keep_one * taps_short[1] * before_one
        + keep_two * taps_short[2] * before_two
        + short_bias.astype(jnp.float32)
    )
    gate_out = shorted[:, :, :width]
    gate_in = shorted[:, :, width : 2 * width]
    values = shorted[:, :, 2 * width :]
    carried_low = (gate_in * values).astype(jnp.bfloat16)
    carried = lax.all_to_all(
        carried_low.transpose(0, 2, 1), "seq", split_axis=1, concat_axis=2, tiled=True
    ).astype(jnp.float32)

    def make_taps(w_one, b_one, w_two, b_two, w_three):
        return filter_taps(w_one, b_one, w_two, b_two, w_three, first_channel, length).T

    taps, filter_pull = jax.vjp(
        make_taps,
        f1_weight.astype(jnp.float32),
        f1_bias.astype(jnp.float32),
        f2_weight.astype(jnp.float32),
        f2_bias.astype(jnp.float32),
        f3_weight.astype(jnp.float32),
    )
    plan = make_plan(seq_count, tok_count)
    everywhere = jnp.arange(length, dtype=jnp.int32)
    masks = document_masks(bounds, everywhere, length)[:, :, None, :]
    taps_real, taps_imag = spectrum(taps, plan)
    spec_real, spec_imag = spectrum(masks * carried[:, None], plan)
    conv_docs = inverse(
        spec_real * taps_real - spec_imag * taps_imag,
        spec_real * taps_imag + spec_imag * taps_real,
        plan,
    )
    conv = jnp.sum(masks * conv_docs, axis=1)
    skip = filter_skip.astype(jnp.float32)[None, :, None]
    long_low = (conv + skip * carried).astype(jnp.bfloat16)
    long_seq = (
        lax.all_to_all(long_low, "seq", split_axis=2, concat_axis=1, tiled=True)
        .transpose(0, 2, 1)
        .astype(jnp.float32)
    )
    mixed_low = (gate_out * long_seq).astype(jnp.bfloat16).reshape(flat_count, width)
    branch = jnp.dot(mixed_low, out_weight, preferred_element_type=jnp.float32) + out_bias.astype(
        jnp.float32
    )
    resid = x_in + branch
    n2, ln2_pull = jax.vjp(
        layer_norm, resid, ln2_gain.astype(jnp.float32), ln2_bias.astype(jnp.float32)
    )
    n2_low = n2.astype(jnp.bfloat16)
    pre = jnp.dot(n2_low, up_weight, preferred_element_type=jnp.float32) + up_bias.astype(
        jnp.float32
    )
    act, gelu_pull = jax.vjp(gelu_tanh, pre)
    act_low = act.astype(jnp.bfloat16)
    result = (
        resid
        + jnp.dot(act_low, down_weight, preferred_element_type=jnp.float32)
        + down_bias.astype(jnp.float32)
    )
    output = result.astype(jnp.bfloat16).reshape(row_count, tok_count, width)
    grad_low = cotangent.reshape(flat_count, width)
    grad_float = grad_low.astype(jnp.float32)
    g_down_w = left_product(act_low, grad_low)
    g_down_b = jnp.sum(grad_float, axis=0)
    g_act = back_product(grad_low, down_weight)
    (g_pre,) = gelu_pull(g_act)
    g_pre_low = g_pre.astype(jnp.bfloat16)
    g_up_w = left_product(n2_low, g_pre_low)
    g_up_b = jnp.sum(g_pre_low.astype(jnp.float32), axis=0)
    g_n2 = back_product(g_pre_low, up_weight)
    g_resid_part, g_ln2_gain, g_ln2_bias = ln2_pull(g_n2)
    g_resid = grad_float + g_resid_part
    g_branch_low = g_resid.astype(jnp.bfloat16)
    g_out_w = left_product(mixed_low, g_branch_low)
    g_out_b = jnp.sum(g_branch_low.astype(jnp.float32), axis=0)
    g_mixed = back_product(g_branch_low, out_weight).reshape(row_count, tok_count, width)
    g_gate_out = g_mixed * long_seq
    g_long_low = (g_mixed * gate_out).astype(jnp.bfloat16)
    g_long = lax.all_to_all(
        g_long_low.transpose(0, 2, 1), "seq", split_axis=1, concat_axis=2, tiled=True
    ).astype(jnp.float32)
    g_skip = jnp.sum(g_long * carried, axis=(0, 2))
    grad_real, grad_imag = spectrum(masks * g_long[:, None], plan)
    back_docs = inverse(
        taps_real * grad_real + taps_imag * grad_imag,
        taps_real * grad_imag - taps_imag * grad_real,
        plan,
    )
    g_carried = jnp.sum(masks * back_docs, axis=1) + skip * g_long
    cross_real = jnp.sum(grad_real * spec_real + grad_imag * spec_imag, axis=(0, 1))
    cross_imag = jnp.sum(grad_imag * spec_real - grad_real * spec_imag, axis=(0, 1))
    g_taps = inverse(cross_real, cross_imag, plan)
    g_f1_w, g_f1_b, g_f2_w, g_f2_b, g_f3_w = filter_pull(g_taps)
    filter_sums = lax.psum((g_f1_w, g_f1_b, g_f2_w, g_f2_b), ("rows", "seq"))
    channel_sums = lax.psum((g_f3_w, g_skip), "rows")
    g_carried_low = g_carried.astype(jnp.bfloat16)
    g_carried_seq = (
        lax.all_to_all(g_carried_low, "seq", split_axis=2, concat_axis=1, tiled=True)
        .transpose(0, 2, 1)
        .astype(jnp.float32)
    )
    g_shorted = jnp.concatenate(
        [g_gate_out, g_carried_seq * values, g_carried_seq * gate_in], axis=-1
    )
    lead_one = keep_one * g_shorted
    lead_two = keep_two * g_shorted
    ahead = passed_along(
        jnp.concatenate([lead_one[:, :2], lead_two[:, :2]], axis=1).astype(jnp.bfloat16), "seq", -1
    ).astype(jnp.float32)
    after_one = jnp.concatenate([lead_one[:, 1:], ahead[:, :1]], axis=1)
    after_two = jnp.concatenate([lead_two[:, 2:], ahead[:, 2:4]], axis=1)
    g_proj = taps_short[0] * g_shorted + taps_short[1] * after_one + taps_short[2] * after_two
    g_short_w = jnp.stack(
        [
            jnp.sum(g_shorted * current, axis=(0, 1)),
            jnp.sum(lead_one * before_one, axis=(0, 1)),
            jnp.sum(lead_two * before_two, axis=(0, 1)),
        ],
        axis=0,
    )
    g_short_b = jnp.sum(g_shorted, axis=(0, 1))
    g_proj_low = g_proj.astype(jnp.bfloat16).reshape(flat_count, 3 * width)
    g_in_w = left_product(n1_low, g_proj_low)
    g_in_b = jnp.sum(g_proj_low.astype(jnp.float32), axis=0)
    g_n1 = back_product(g_proj_low, in_weight)
    g_x_part, g_ln1_gain, g_ln1_bias = ln1_pull(g_n1)
    grad_tokens = (g_resid + g_x_part).reshape(row_count, tok_count, width)
    every_sum = (
        lax.psum_scatter(g_ln2_gain, ("rows", "seq"), scatter_dimension=0, tiled=True),
        lax.psum_scatter(g_ln2_bias, ("rows", "seq"), scatter_dimension=0, tiled=True),
        lax.psum_scatter(g_up_w, ("rows", "seq"), scatter_dimension=0, tiled=True),
        lax.psum_scatter(g_up_b, ("rows", "seq"), scatter_dimension=0, tiled=True),
        lax.psum_scatter(g_down_w, ("rows", "seq"), scatter_dimension=0, tiled=True),
        lax.psum_scatter(g_down_b, ("rows", "seq"), scatter_dimension=0, tiled=True),
        lax.psum_scatter(g_ln1_gain, ("rows", "seq"), scatter_dimension=0, tiled=True),
        lax.psum_scatter(g_ln1_bias, ("rows", "seq"), scatter_dimension=0, tiled=True),
        lax.psum_scatter(g_in_w, ("rows", "seq"), scatter_dimension=0, tiled=True),
        lax.psum_scatter(g_in_b, ("rows", "seq"), scatter_dimension=0, tiled=True),
        lax.psum_scatter(g_short_w.T, ("rows", "seq"), scatter_dimension=0, tiled=True),
        lax.psum_scatter(g_short_b, ("rows", "seq"), scatter_dimension=0, tiled=True),
        lax.psum_scatter(g_out_w, ("rows", "seq"), scatter_dimension=0, tiled=True),
        lax.psum_scatter(g_out_b, ("rows", "seq"), scatter_dimension=0, tiled=True),
    )
    ffn_sums = every_sum[:6]
    mixer_sums = every_sum[6:]
    return (
        output,
        grad_tokens,
        mixer_sums[0],
        mixer_sums[1],
        mixer_sums[2],
        mixer_sums[3],
        mixer_sums[4].T,
        mixer_sums[5],
        filter_sums[0],
        filter_sums[1],
        filter_sums[2],
        filter_sums[3],
        channel_sums[0],
        channel_sums[1],
        mixer_sums[6],
        mixer_sums[7],
        ffn_sums[0],
        ffn_sums[1],
        ffn_sums[2],
        ffn_sums[3],
        ffn_sums[4],
        ffn_sums[5],
    )


def solution(mesh):
    return jax.shard_map(
        per_device,
        mesh=mesh,
        in_specs=(
            P("rows", "seq", None),
            P("rows", "seq", None),
            P("rows", None),
            P(),
            P(),
            P(),
            P(),
            P(),
            P(),
            P(),
            P(),
            P(),
            P(),
            P(None, "seq"),
            P("seq"),
            P(),
            P(),
            P(),
            P(),
            P(),
            P(),
            P(),
            P(),
        ),
        out_specs=(
            P("rows", "seq", None),
            P("rows", "seq", None),
            P(("rows", "seq")),
            P(("rows", "seq")),
            P(("rows", "seq"), None),
            P(("rows", "seq")),
            P(None, ("rows", "seq")),
            P(("rows", "seq")),
            P(),
            P(),
            P(),
            P(),
            P(None, "seq"),
            P("seq"),
            P(("rows", "seq"), None),
            P(("rows", "seq")),
            P(("rows", "seq")),
            P(("rows", "seq")),
            P(("rows", "seq"), None),
            P(("rows", "seq")),
            P(("rows", "seq"), None),
            P(("rows", "seq")),
        ),
        check_vma=False,
    )
```

profile of v0, /device:TPU:0, one launch (start us, length us, event | category | flops | bytes accessed | tf_op | source)
XLA Modules:
  0.0 1786.9 jit_solution(7663502642461187351)
XLA Ops:
  118.1 16.7 fusion.2
  134.8 19.2 %fusion.44 = f32[2,3,128,16,256]{4,2,3,1,0:T(8,128)} fusion(f32[2,3,128,16,256]{4,3,2,1,0:T(8,128)S(1)} %get-tuple-element.69), kind=kOutput, calls=%fused_computation.60 | convolution fusion | flops 9664593920 | bytes 25165824 | tf_op jit(solution)/shard_map/...km,mj->...kj/dot_general | solution.py:86
  154.0 19.2 %fusion.46 = f32[2,3,128,16,256]{4,2,3,1,0:T(8,128)} fusion(f32[2,3,128,16,256]{4,3,2,1,0:T(8,128)S(1)} %get-tuple-element.69), kind=kOutput, calls=%fused_computation.62 | convolution fusion | flops 9664593920 | bytes 25165824 | tf_op jit(solution)/shard_map/...km,mj->...kj/dot_general | solution.py:86
  173.2 26.4 %fusion.88 = f32[2,3,128,16,256]{4,2,3,1,0:T(8,128)} fusion(f32[2,3,128,16,256]{4,2,3,1,0:T(8,128)} %fusion.46, f32[2,3,128,16,256]{4,3,2,1,0:T(8,128)} %get-tuple-element.68), kind=kOutput, calls=%fused_computation.123 | convolution fusion | flops 9667739648 | bytes 37748736 | tf_op jit(solution)/shard_map/...km,mj->...kj/dot_general | solution.py:86
  199.6 33.0 %multiply_subtract_fusion.1 = (f32[2,3,128,16,256]{4,2,3,1,0:T(8,128)}, f32[2,3,128,16,256]{4,2,3,1,0:T(8,128)}, f32[2,3,128,16,256]{4,2,3,1,0:T(8,128)}) fusion(f32[2,3,128,16,256]{4,2,3,1,0:T(8,128)} %fusion.88, f32[128,16,256]{2,0,1:T(8,128)S(1)} %copy-done.2, f32[128,16,256]{2,0,1:T(8,128)S(1)} %copy-done.4, f32[2,3,128,16,256]{4,2,3,1,0:T(8,128)} %fusion.44, ...), kind=kOutput, calls=%fused_computation.33 | convolution fusion | flops 9686614016 | bytes 79691776 | tf_op jit(solution)/shard_map/...km,mj->...kj/dot_general | solution.py:86
  232.6 25.0 %fusion.32 = f32[2,3,128,16,256]{4,3,2,1,0:T(8,128)} fusion(f32[2,3,128,16,256]{4,2,3,1,0:T(8,128)} %get-tuple-element.64), kind=kOutput, calls=%fused_computation.48 | convolution fusion | flops 9664593920 | bytes 25165824 | tf_op jit(solution)/shard_map/...km,mj->...kj/dot_general | solution.py:86
  257.7 24.9 %fusion.34 = f32[2,3,128,16,256]{4,3,2,1,0:T(8,128)} fusion(f32[2,3,128,16,256]{4,2,3,1,0:T(8,128)} %get-tuple-element.64), kind=kOutput, calls=%fused_computation.50 | convolution fusion | flops 9664593920 | bytes 25165824 | tf_op jit(solution)/shard_map/...km,mj->...kj/dot_general | solution.py:86
  282.6 19.4 %fusion.28 = f32[2,3,128,16,256]{4,3,2,1,0:T(8,128)} fusion(f32[2,3,128,16,256]{4,2,3,1,0:T(8,128)S(1)} %bitcast.323), kind=kOutput, calls=%fused_computation.44 | convolution fusion | flops 9664593920 | bytes 25165824 | tf_op jit(solution)/shard_map/...km,mj->...kj/dot_general | solution.py:86
  302.0 19.2 %fusion.30 = f32[2,3,128,16,256]{4,3,2,1,0:T(8,128)} fusion(f32[2,3,128,16,256]{4,2,3,1,0:T(8,128)S(1)} %bitcast.323), kind=kOutput, calls=%fused_computation.46 | convolution fusion | flops 9664593920 | bytes 25165824 | tf_op jit(solution)/shard_map/...km,mj->...kj/dot_general | solution.py:86
  321.3 21.5 %fusion.12 = f32[2,3,128,256,8]{3,4,2,1,0:T(8,128)} fusion(f32[16,256]{1,0:T(8,128)S(1)} %get-tuple-element.110, f32[16,256]{1,0:T(8,128)S(1)} %get-tuple-element.111, f32[2,3,128,16,256]{4,3,2,1,0:T(8,128)} %fusion.28, f32[2,3,128,16,256]{4,3,2,1,0:T(8,128)} %fusion.32, f32[2,3,128,16,256]{4,3,2,1,0:T(8,128)} %fusion.34, ...), kind=kOutput, calls=%fused_computation.24 | convolution fusion | flops 317718528 | bytes 56656896 | tf_op jit(solution)/shard_map/nk,...km->...nm/dot_general | solution.py:107
  342.7 22.1 %fusion.71 = f32[2,128,8,256]{3,2,1,0:T(8,128)} fusion(f32[2,3,128,256,8]{3,4,2,1,0:T(8,128)} %fusion.12, f32[2,3,8,256]{3,2,1,0:T(8,128)S(1)} %copy-done.39, f32[16,256]{1,0:T(8,128)S(1)} %get-tuple-element.110, f32[16,256]{1,0:T(8,128)S(1)} %get-tuple-element.111, f32[2,3,128,16,256]{4,3,2,1,0:T(8,128)} %fusion.28, f32[2,3,128,16,256]{4,3,2,1,0:T(8,128)} %fusion.32, ...), kind=kOutput, calls=%fused_computation.98 | convolution fusion | flops 321912832 | bytes 58803200 | tf_op jit(solution)/shard_map/nk,...km->...nm/dot_general | solution.py:107
  383.6 15.2 all-to-all-done.1
  496.8 16.6 fusion
  513.4 19.2 %fusion.36 = f32[2,3,128,16,256]{4,2,3,1,0:T(8,128)} fusion(f32[2,3,128,16,256]{4,3,2,1,0:T(8,128)S(1)} %get-tuple-element.67), kind=kOutput, calls=%fused_computation.52 | convolution fusion | flops 9664593920 | bytes 25165824 | tf_op jit(solution)/shard_map/...km,mj->...kj/dot_general | solution.py:86
  532.6 19.2 %fusion.38 = f32[2,3,128,16,256]{4,2,3,1,0:T(8,128)} fusion(f32[2,3,128,16,256]{4,3,2,1,0:T(8,128)S(1)} %get-tuple-element.67), kind=kOutput, calls=%fused_computation.54 | convolution fusion | flops 9664593920 | bytes 25165824 | tf_op jit(solution)/shard_map/...km,mj->...kj/dot_general | solution.py:86
  551.8 26.2 %fusion.94 = f32[2,3,128,16,256]{4,2,3,1,0:T(8,128)} fusion(f32[2,3,128,16,256]{4,2,3,1,0:T(8,128)} %fusion.38, f32[2,3,128,16,256]{4,3,2,1,0:T(8,128)} %get-tuple-element.66), kind=kOutput, calls=%fused_computation.125 | convolution fusion | flops 9667739648 | bytes 37748736 | tf_op jit(solution)/shard_map/...km,mj->...kj/dot_general | solution.py:86
  578.0 40.0 %add_reduce_fusion = (f32[128,16,256]{2,0,1:T(8,128)}, f32[128,16,256]{2,0,1:T(8,128)}, f32[2,3,128,16,256]{4,2,3,1,0:T(8,128)}, f32[2,3,128,16,256]{4,2,3,1,0:T(8,128)}) fusion(f32[2,3,128,16,256]{4,2,3,1,0:T(8,128)} %get-tuple-element.99, f32[2,3,128,16,256]{4,2,3,1,0:T(8,128)} %fusion.94, f32[2,3,128,16,256]{4,2,3,1,0:T(8,128)} %fusion.88, ...), kind=kOutput, calls=%fused_computation.13 | convolution fusion | flops 9710731264 | bytes 96468992 | tf_op jit(solution)/shard_map/...km,mj->...kj/dot_general | solution.py:86
  628.8 25.1 %fusion.20 = f32[2,3,128,16,256]{4,3,2,1,0:T(8,128)} fusion(f32[2,3,128,16,256]{4,2,3,1,0:T(8,128)} %get-tuple-element.70), kind=kOutput, calls=%fused_computation.36 | convolution fusion | flops 9664593920 | bytes 25165824 | tf_op jit(solution)/shard_map/...km,mj->...kj/dot_general | solution.py:86
  653.9 25.1 %fusion.22 = f32[2,3,128,16,256]{4,3,2,1,0:T(8,128)} fusion(f32[2,3,128,16,256]{4,2,3,1,0:T(8,128)} %get-tuple-element.70), kind=kOutput, calls=%fused_computation.38 | convolution fusion | flops 9664593920 | bytes 25165824 | tf_op jit(solution)/shard_map/...km,mj->...kj/dot_general | solution.py:86
  679.0 19.7 %fusion.24 = f32[2,3,128,16,256]{4,3,2,1,0:T(8,128)} fusion(f32[2,3,128,16,256]{4,2,3,1,0:T(8,128)S(1)} %bitcast.321), kind=kOutput, calls=%fused_computation.40 | convolution fusion | flops 9664593920 | bytes 25165824 | tf_op jit(solution)/shard_map/...km,mj->...kj/dot_general | solution.py:86
  698.7 19.1 %fusion.26 = f32[2,3,128,16,256]{4,3,2,1,0:T(8,128)} fusion(f32[2,3,128,16,256]{4,2,3,1,0:T(8,128)S(1)} %bitcast.321), kind=kOutput, calls=%fused_computation.42 | convolution fusion | flops 9664593920 | bytes 25165824 | tf_op jit(solution)/shard_map/...km,mj->...kj/dot_general | solution.py:86
  728.8 21.7 %fusion.4 = f32[2,3,128,256,8]{3,4,2,1,0:T(8,128)} fusion(f32[16,256]{1,0:T(8,128)S(1)} %get-tuple-element.110, f32[16,256]{1,0:T(8,128)S(1)} %get-tuple-element.111, f32[2,3,128,16,256]{4,3,2,1,0:T(8,128)} %fusion.20, f32[2,3,128,16,256]{4,3,2,1,0:T(8,128)} %fusion.24, f32[2,3,128,16,256]{4,3,2,1,0:T(8,128)} %fusion.26, ...), kind=kOutput, calls=%fused_computation.14 | convolution fusion | flops 317718528 | bytes 56656896 | tf_op jit(solution)/shard_map/nk,...km->...nm/dot_general | solution.py:107
  750.5 22.1 %fusion.70 = f32[2,128,8,256]{3,2,1,0:T(8,128)} fusion(f32[2,3,128,256,8]{3,4,2,1,0:T(8,128)} %fusion.4, f32[2,3,8,256]{3,2,1,0:T(8,128)S(1)} %copy-done.40, f32[16,256]{1,0:T(8,128)S(1)} %get-tuple-element.110, f32[16,256]{1,0:T(8,128)S(1)} %get-tuple-element.111, f32[2,3,128,16,256]{4,3,2,1,0:T(8,128)} %fusion.20, f32[2,3,128,16,256]{4,3,2,1,0:T(8,128)} %fusion.24, ...), kind=kOutput, calls=%fused_computation.96 | convolution fusion | flops 321912832 | bytes 58803200 | tf_op jit(solution)/shard_map/nk,...km->...nm/dot_general | solution.py:107
  813.4 19.5 %multiply_reduce_fusion.2 = (f32[3072]{0:T(1024)S(1)}, f32[3072]{0:T(1024)S(1)}, f32[3072]{0:T(1024)S(1)}, f32[3072]{0:T(1024)}, f32[2,256,3072]{1,2,0:T(8,128)}, /*index=5*/f32[2,256,3072]{1,2,0:T(8,128)}) fusion(f32[2,258,3072]{1,2,0:T(8,128)} %copy-done.5, f32[2,256,1024]{1,2,0:T(8,128)} %get-tuple-element.73, f32[2,256,1024]{1,2,0:T(8,128)S(1)} %get-tuple-element.72, ...), kind=kLoop, calls=%fused_computation.101 | loop fusion | flops 17289216 | bytes 37801984 | tf_op jit(solution)/shard_map/reduce_sum | solution.py:290
  869.8 17.6 convert_reduce_fusion.1
  931.4 15.6 fusion.405
  974.6 20.4 %all-reduce.12 = (f32[64,128]{1,0:T(8,128)}, f32[128]{0:T(128)}) all-reduce(f32[64,128]{1,0:T(8,128)S(1)} %fusion.189, f32[128]{0:T(128)S(1)} %multiply_reduce_fusion.4), channel_id=1, replica_groups=mesh['rows'=4,'seq'=8] {'rows'}, use_global_device_ids=true, to_apply=%region_32.33 | all-reduce | flops 8320 | bytes 66560 | tf_op jit(solution)/shard_map/psum | solution.py:270
  1001.3 99.3 %all-reduce.15.cloned.1.call-done = (f32[1024]{0:T(1024)}, f32[1024]{0:T(1024)}, f32[3072]{0:T(1024)}, f32[3072]{0:T(1024)}, f32[33,64]{1,0:T(8,128)}, /*index=5...) async-done(((f32[1024]{0:T(1024)}, f32[1024]{0:T(1024)}, ...) | async-done | bytes 90896
  1111.9 132.0 %reduce-scatter.10.cloned.1.call-done = f32[32,1024]{1,0:T(8,128)} async-done(((f32[1024,1024]{1,0:T(8,128)}), f32[32,1024]{1,0:T(8,128)}) %reduce-scatter.10.cloned.1.call-update) | async-done | bytes 131088 | tf_op jit(solution)/shard_map/reduce_scatter | solution.py:316
  1243.9 158.9 %reduce-scatter.8.cloned.1.call-done = f32[32,3072]{1,0:T(8,128)} async-done(((f32[1024,3072]{1,0:T(8,128)}), f32[32,3072]{1,0:T(8,128)}) %reduce-scatter.8.cloned.1.call-update) | async-done | bytes 393232 | tf_op jit(solution)/shard_map/reduce_scatter | solution.py:312
  1402.8 184.6 %reduce-scatter.14.cloned.1.call-done = f32[128,1024]{1,0:T(8,128)} async-done(((f32[4096,1024]{1,0:T(8,128)}), f32[128,1024]{1,0:T(8,128)}) %reduce-scatter.14.cloned.1.call-update) | async-done | bytes 524304 | tf_op jit(solution)/shard_map/reduce_scatter | solution.py:308
  1587.4 187.2 %reduce-scatter.12.cloned.1.call-done = f32[32,4096]{1,0:T(8,128)} async-done(((f32[1024,4096]{1,0:T(8,128)}), f32[32,4096]{1,0:T(8,128)}) %reduce-scatter.12.cloned.1.call-update) | async-done | bytes 524304 | tf_op jit(solution)/shard_map/reduce_scatter | solution.py:306
  (395 shorter events, 420.1 us)
Async XLA Ops:
  7.2 402.0 %copy-start = (bf16[1024,1024]{1,0:T(8,128)(2,1)S(1)}, bf16[1024,1024]{1,0:T(8,128)(2,1)}, u32[]{:S(2)}) copy-start(bf16[1024,1024]{1,0:T(8,128)(2,1)} %param.38) | copy-start | bytes 6291460
  23.0 36.1 %collective-permute-start = (bf16[2,2,3072]{2,1,0:T(2,128)(2,1)S(1)}, bf16[2,2,3072]{2,1,0:T(2,128)(2,1)S(1)}, u32[]{:S(2)}, u32[]{:S(2)}) collective-permute-start(bf16[2,2,3072]{2,1,0:T(2,128)(2,1)S(1)} %slice.110), channel_id=1, source_target_pairs={{0,1},{1,2},{2,3},{3,4},{4,5},{5,6},{6,7},{8,9},{9,10},{10,11},{11... | collective-permute-start | bytes 73736 | tf_op jit(solution)/shard_map/ppermute | solution.py:21
  53.9 64.2 %copy-start.33 = (f32[2,3,8,256]{3,2,1,0:T(8,128)}, f32[2,3,8,256]{3,2,1,0:T(8,128)S(1)}, u32[]{:S(2)}) copy-start(f32[2,3,8,256]{3,2,1,0:T(8,128)S(1)} %fusion.253) | copy-start | bytes 147460
  75.3 20.4 %all-to-all-start = ((bf16[2,1024,256]{2,0,1:T(2,128)(2,1)}), bf16[2,1024,256]{2,0,1:T(2,128)(2,1)S(1)}, u32[]{:S(2)}, u32[]{:S(2)}) async-start(bf16[2,1024,256]{2,0,1:T(2,128)(2,1)} %copy.275), calls=%async_computation | async-start | bytes 2097152 | tf_op jit(solution)/shard_map/all_to_all | solution.py:183
  173.2 26.4 %copy-start.2 = (f32[128,16,256]{2,0,1:T(8,128)S(1)}, f32[128,16,256]{2,0,1:T(8,128)}, u32[]{:S(2)}) copy-start(f32[128,16,256]{2,0,1:T(8,128)} %fusion.162) | copy-start | bytes 6291460
  173.2 26.4 %copy-start.4 = (f32[128,16,256]{2,0,1:T(8,128)S(1)}, f32[128,16,256]{2,0,1:T(8,128)}, u32[]{:S(2)}) copy-start(f32[128,16,256]{2,0,1:T(8,128)} %fusion.159) | copy-start | bytes 6291460
  232.6 50.0 %slice-start.3 = ((s8[12582912]{0:T(1024)(128)(4,1)}), s8[4194304]{0:T(1024)(128)(4,1)S(1)}, s32[]{:S(2)}) async-start(s8[12582912]{0:T(1024)(128)(4,1)} %bitcast.322), calls=%async_computation.18 | async-start | bytes 8388608
  232.6 50.0 %slice-start.4 = ((s8[12582912]{0:T(1024)(128)(4,1)}), s8[4194304]{0:T(1024)(128)(4,1)S(1)}, s32[]{:S(2)}) async-start(s8[12582912]{0:T(1024)(128)(4,1)} %bitcast.322), calls=%async_computation.19 | async-start | bytes 8388608
  342.7 25.1 %copy-start.95 = (f32[128]{0:T(128)S(1)}, f32[128]{0:T(128)}, u32[]{:S(2)}) copy-start(f32[128]{0:T(128)} %convert_element_type.410) | copy-start | bytes 1540
  379.7 19.1 %all-to-all-start.1 = ((bf16[2,128,2048]{1,0,2:T(2,128)(2,1)}), bf16[2,128,2048]{1,0,2:T(2,128)(2,1)S(1)}, u32[]{:S(2)}, u32[]{:S(2)}) async-start(bf16[2,128,2048]{1,0,2:T(2,128)(2,1)} %copy.296), calls=%async_computation.1 | async-start | bytes 2097152 | tf_op jit(solution)/shard_map/all_to_all | solution.py:212
  383.5 59.1 %copy-start.76 = (f32[1024]{0:T(1024)}, f32[1024]{0:T(1024)S(1)}, u32[]{:S(2)}) copy-start(f32[1024]{0:T(1024)S(1)} %convert_element_type.421) | copy-start | bytes 12292
  383.6 28.6 %copy-start.87 = (f32[1024]{0:T(1024)}, f32[1024]{0:T(1024)S(1)}, u32[]{:S(2)}) copy-start(f32[1024]{0:T(1024)S(1)} %convert_element_type.422) | copy-start | bytes 12292
  383.6 39.3 %copy-start.74 = (f32[4096]{0:T(1024)}, f32[4096]{0:T(1024)S(1)}, u32[]{:S(2)}) copy-start(f32[4096]{0:T(1024)S(1)} %convert_element_type.424) | copy-start | bytes 49156
  411.8 30.9 %copy-start.23 = (f32[512,1024]{1,0:T(8,128)}, f32[512,1024]{1,0:T(8,128)S(1)}, u32[]{:S(2)}) copy-start(f32[512,1024]{1,0:T(8,128)S(1)} %get-tuple-element.101) | copy-start | bytes 6291460
  411.8 30.9 %copy-start.66 = (f32[512]{0:T(512)}, f32[512]{0:T(512)S(1)}, u32[]{:S(2)}) copy-start(f32[512]{0:T(512)S(1)} %broadcast_multiply_fusion.2) | copy-start | bytes 6148
  412.2 30.5 %copy-start.81 = (f32[512]{0:T(512)}, f32[512]{0:T(512)S(1)}, u32[]{:S(2)}) copy-start(f32[512]{0:T(512)S(1)} %fusion.297) | copy-start | bytes 6148
  456.5 19.9 %all-to-all-start.2 = ((bf16[2,1024,256]{2,0,1:T(2,128)(2,1)}), bf16[2,1024,256]{2,0,1:T(2,128)(2,1)}, u32[]{:S(2)}, u32[]{:S(2)}) async-start(bf16[2,1024,256]{2,0,1:T(2,128)(2,1)} %copy.303), calls=%async_computation.2 | async-start | bytes 2097152 | tf_op jit(solution)/shard_map/all_to_all | solution.py:254
  551.8 26.3 %copy-start.3 = (f32[128,16,256]{2,0,1:T(8,128)S(1)}, f32[128,16,256]{2,0,1:T(8,128)}, u32[]{:S(2)}) copy-start(f32[128,16,256]{2,0,1:T(8,128)} %fusion.162) | copy-start | bytes 6291460
  628.8 50.2 %slice-start = ((s8[12582912]{0:T(1024)(128)(4,1)}), s8[4194304]{0:T(1024)(128)(4,1)S(1)}, s32[]{:S(2)}) async-start(s8[12582912]{0:T(1024)(128)(4,1)} %bitcast.320), calls=%async_computation.15 | async-start | bytes 8388608
  628.8 50.2 %slice-start.1 = ((s8[12582912]{0:T(1024)(128)(4,1)}), s8[4194304]{0:T(1024)(128)(4,1)S(1)}, s32[]{:S(2)}) async-start(s8[12582912]{0:T(1024)(128)(4,1)} %bitcast.320), calls=%async_computation.16 | async-start | bytes 8388608
  728.8 62.8 %copy-start.18 = (f32[16,8,8,256]{3,1,2,0:T(8,128)}, f32[16,8,8,256]{3,1,2,0:T(8,128)S(1)}, u32[]{:S(2)}) copy-start(f32[16,8,8,256]{3,1,2,0:T(8,128)S(1)} %copy.379) | copy-start | bytes 3145732
  750.5 25.1 %copy-start.96 = (f32[128]{0:T(128)S(1)}, f32[128]{0:T(128)}, u32[]{:S(2)}) copy-start(f32[128]{0:T(128)} %convert_element_type.410) | copy-start | bytes 1540
  787.6 18.9 %all-to-all-start.3 = ((bf16[2,128,2048]{1,0,2:T(2,128)(2,1)}), bf16[2,128,2048]{1,0,2:T(2,128)(2,1)S(1)}, u32[]{:S(2)}, u32[]{:S(2)}) async-start(bf16[2,128,2048]{1,0,2:T(2,128)(2,1)} %copy.318), calls=%async_computation.3 | async-start | bytes 2097152 | tf_op jit(solution)/shard_map/all_to_all | solution.py:273
  791.6 203.4 %reduce-scatter.16.cloned.1.call-start = ((), (), s32[]{:S(2)}) async-start(), calls=%async_computation.13 | async-start | bytes 1622016
  843.0 22.3 %collective-permute-start.1 = (bf16[2,4,3072]{2,1,0:T(4,128)(2,1)S(1)}, bf16[2,4,3072]{2,1,0:T(4,128)(2,1)S(1)}, u32[]{:S(2)}, u32[]{:S(2)}) collective-permute-start(bf16[2,4,3072]{2,1,0:T(4,128)(2,1)S(1)} %pad_maximum_fusion.6), channel_id=1, source_target_pairs={{1,0},{2,1},{3,2},{4,3},{5,4},{6,5},{7,6},{9,8},{10,9},{11,10},{12... | collective-permute-start | bytes 147464 | tf_op jit(solution)/shard_map/ppermute | solution.py:21
  865.2 235.3 %all-reduce.15.cloned.1.call-start = ((), (), s32[]{:S(2)}) async-start(), calls=%async_computation.14 | async-start | bytes 239616
  916.3 327.7 %reduce-scatter.10.cloned.1.call-start = ((), (), s32[]{:S(2)}) async-start(), calls=%async_computation.10 | async-start | bytes 4325376 | tf_op jit(solution)/shard_map/reduce_scatter | solution.py:316
  921.3 481.5 %reduce-scatter.8.cloned.1.call-start = ((), (), s32[]{:S(2)}) async-start(), calls=%async_computation.9 | async-start | bytes 12976128 | tf_op jit(solution)/shard_map/reduce_scatter | solution.py:312
  930.2 657.2 %reduce-scatter.14.cloned.1.call-start = ((), (), s32[]{:S(2)}) async-start(), calls=%async_computation.12 | async-start | bytes 17301504 | tf_op jit(solution)/shard_map/reduce_scatter | solution.py:308
  947.1 827.5 %reduce-scatter.12.cloned.1.call-start = ((), (), s32[]{:S(2)}) async-start(), calls=%async_computation.11 | async-start | bytes 17301504 | tf_op jit(solution)/shard_map/reduce_scatter | solution.py:306
  959.9 36.6 %copy-start.63 = (f32[512]{0:T(512)S(1)}, f32[512]{0:T(512)}, u32[]{:S(2)}) copy-start(f32[512]{0:T(512)} %copy-done.62) | copy-start | bytes 6148
  959.9 819.7 %copy-start.1 = (bf16[1024,1024]{1,0:T(8,128)(2,1)S(1)}, bf16[1024,1024]{1,0:T(8,128)(2,1)}, u32[]{:S(2)}) copy-start(bf16[1024,1024]{1,0:T(8,128)(2,1)} %param.38) | copy-start | bytes 6291460
  (89 other events, 930.7 us)
Sparse Core Ops, SparseCore 0:
  865.3 98.0 reduce-scatter.15
  971.0 129.4 all-reduce.14
  1103.5 140.4 reduce-scatter.9
  1251.4 151.3 reduce-scatter.7
  1405.5 181.8 reduce-scatter.13
  1590.1 184.3 reduce-scatter.11
where the time goes:
time: 1790 us
  waiting for transfers between devices  797 us (45%)
  matrix products  699 us (39%)
  local copies, waits for them, and re-layouts  138 us (8%)
  other arithmetic  95.5 us (5%)
  starting transfers between devices  21.7 us (1%)
  blocking collectives  20.4 us (1%)
    dot_general x24, matrix products, right_mul(): return jnp.einsum('...km,mj->...kj', left, table, precision=HIGH)  422 us
    reduce_scatter x1, waiting for transfers between devices, per_device(): lax.psum_scatter(g_up_w, ('rows', 'seq'), scatter_dimension=0, tiled=True)  187 us
    reduce_scatter x1, waiting for transfers between devices, per_device(): lax.psum_scatter(g_down_w, ('rows', 'seq'), scatter_dimension=0, tiled=True)  185 us
    reduce_scatter x1, waiting for transfers between devices, per_device(): lax.psum_scatter(g_in_w, ('rows', 'seq'), scatter_dimension=0, tiled=True)  159 us
    reduce_scatter x1, waiting for transfers between devices, per_device(): lax.psum_scatter(g_out_w, ('rows', 'seq'), scatter_dimension=0, tiled=True)  132 us
    unnamed x8, waiting for transfers between devices  99.4 us
    dot_general x3, matrix products, inverse(): jnp.einsum('nk,...km->...nm', cos_outer[:blocks], real_u, precision=HIGH)  45.6 us
    dot_general x3, matrix products, inverse(): jnp.einsum('nk,...km->...nm', sin_outer[:blocks], imag_u, precision=HIGH)  44.6 us
  transfers between devices with their start and end apart: 12, of which 9 were waited for; matrix products, arithmetic and copies ran while one was open for 11% of the time, Pallas kernels for 0%

commit v1 on v0

v1 whole, which is shorter than its diff:
```python
import functools
import math

import jax
import jax.numpy as jnp
import ml_dtypes
import numpy as np
from jax import lax
from jax.experimental import pallas as pl
from jax.experimental.pallas import tpu as pltpu
from jax.sharding import PartitionSpec as P

D = 1024
EMB = 33
HIGH = lax.Precision.HIGHEST
eps = 1e-05
slow_rate = math.log(100.0) / 1.5
fast_rate = math.log(100.0) / 0.3
BOTH = ("rows", "seq")
F32 = jnp.float32
BF16 = jnp.bfloat16
VMEM_LIMIT = 56 * 1024 * 1024


def passed_along(value, axis, steps):
    count = lax.axis_size(axis)
    first, last = (max(0, -steps), min(count, count - steps))
    return lax.ppermute(value, axis, [(source, source + steps) for source in range(first, last)])


def layer_norm(values, gain, shift):
    center = values - jnp.mean(values, axis=-1, keepdims=True)
    spread = jnp.mean(center * center, axis=-1, keepdims=True)
    return center * lax.rsqrt(spread + eps) * gain + shift


def gelu_tanh(values):
    return jax.nn.gelu(values, approximate=True)


def features(length):
    steps = np.arange(length, dtype=np.float64)
    bands = (EMB - 1) // 2
    freqs = 0.0001 + np.arange(bands, dtype=np.float64) * ((bands - 1 - 0.0001) / (bands - 1))
    angles = (steps * (2.0 * math.pi / length))[:, None] * freqs[None, :]
    timeline = steps / (length - 1)
    table = np.concatenate([timeline[:, None], np.cos(angles), -np.sin(angles)], axis=1)
    return jnp.asarray(table.astype(np.float32)), jnp.asarray(timeline.astype(np.float32))


def filter_taps(w_one, b_one, w_two, b_two, w_three, first, length):
    feats, timeline = features(length)
    hidden = jnp.sin(jnp.dot(feats, w_one, precision=HIGH) + b_one)
    hidden = jnp.sin(jnp.dot(hidden, w_two, precision=HIGH) + b_two)
    raw_taps = jnp.dot(hidden, w_three, precision=HIGH)
    channels = (first + jnp.arange(w_three.shape[1], dtype=jnp.int32)).astype(F32)
    rates = slow_rate + channels * ((fast_rate - slow_rate) / (D - 1))
    return raw_taps * jnp.exp(-timeline[:, None] * rates[None, :])


def split16(values):
    high = values.astype(ml_dtypes.bfloat16)
    return high, (values - high.astype(np.float64)).astype(ml_dtypes.bfloat16)


def transform_tables(block):
    freq = np.arange(block)[:, None]
    time = np.arange(block)[None, :]
    angles = ((2 * freq + 1) * time % (4 * block)) * (math.pi / (2 * block))
    ahead = np.concatenate([np.cos(angles), -np.sin(angles)], axis=0)
    ahead_high, ahead_low = split16(ahead)
    back_high, back_low = split16(ahead.T / block)
    return tuple(jnp.asarray(t) for t in (ahead_high, ahead_low, back_high, back_low))


def piece_table(bounds, blocks, block):
    length = blocks * block
    edges = jnp.broadcast_to(jnp.arange(blocks, dtype=jnp.int32) * block, (bounds.shape[0], blocks))
    for cut in range(bounds.shape[1]):
        one = bounds[:, cut : cut + 1]
        low = jnp.concatenate([jnp.full_like(one, -1), edges], axis=1)
        high = jnp.concatenate([edges, jnp.full_like(one, length)], axis=1)
        edges = jnp.maximum(low, jnp.minimum(one, high))
    ends = jnp.concatenate([edges[:, 1:], jnp.full_like(edges[:, :1], length)], axis=1)
    index = jnp.minimum(edges // block, blocks - 1)
    start = jnp.max(
        jnp.where(bounds[:, :, None] <= edges[:, None, :], bounds[:, :, None], 0), axis=1
    )
    stop = jnp.min(
        jnp.where(bounds[:, :, None] > edges[:, None, :], bounds[:, :, None], length), axis=1
    )
    empty = ends <= edges
    earlier = jnp.where(empty, 0, index - start // block + 1)
    later = jnp.where(empty, 0, (stop - 1) // block - index + 1)
    return jnp.stack([edges, ends, index, earlier, later]).astype(jnp.int32)


def dot32(left, right):
    return jnp.dot(left, right, preferred_element_type=F32)


def split32(values):
    high = values.astype(BF16)
    return high, (values - high.astype(F32)).astype(BF16)


def wide_dot(high, low, values):
    top, rest = split32(values)
    return dot32(high, top) + dot32(high, rest) + dot32(low, top)


def alternating(rows, lanes):
    odd = lax.broadcasted_iota(jnp.int32, (rows, lanes), 0) % 2
    return 1.0 - 2.0 * odd.astype(F32)


def taps_spectrum_kernel(taps_ref, high_ref, low_ref, out_ref, own):
    blocks, block, lanes = taps_ref.shape
    for k in range(blocks):
        own[k] = wide_dot(high_ref[...], low_ref[...], taps_ref[k])
    sign = alternating(block, lanes)
    out_ref[0] = own[0]
    for k in range(1, blocks):
        out_ref[k, :block] = own[k, :block] - sign * own[k - 1, block:]
        out_ref[k, block:] = own[k, block:] + sign * own[k - 1, :block]


def taps_spectrum(taps, tables):
    blocks, block, lanes = taps.shape
    return pl.pallas_call(
        taps_spectrum_kernel,
        out_shape=jax.ShapeDtypeStruct((blocks, 2 * block, lanes), F32),
        scratch_shapes=[pltpu.VMEM((blocks, 2 * block, lanes), F32)],
        compiler_params=pltpu.CompilerParams(vmem_limit_bytes=VMEM_LIMIT),
        name="taps_spectrum",
    )(taps, tables[0], tables[1])


def piece_mask(table_ref, row, piece, block, lanes):
    at = table_ref[2, row, piece]
    spot = lax.broadcasted_iota(jnp.int32, (block, lanes), 0) + at * block
    return at, (spot >= table_ref[0, row, piece]) & (spot < table_ref[1, row, piece])


def piece_spectra(table_ref, series_ref, high_ref, low_ref, out_ref):
    blocks, rows, block, lanes = series_ref.shape
    for piece in range(out_ref.shape[0]):
        parts = []
        for row in range(rows):
            at, inside = piece_mask(table_ref, row, piece, block, lanes)
            values = series_ref[at, row].astype(F32)
            parts.append(jnp.where(inside, values, 0.0).astype(BF16))
        both = jnp.concatenate(parts, axis=1)
        out_ref[piece] = dot32(high_ref[...], both) + dot32(low_ref[...], both)


def couple(count, step, taps_ref, series_ref, piece, row, into_ref, conjugate):
    block = taps_ref.shape[1] // 2
    lanes = taps_ref.shape[2]
    lane = pl.ds(row * lanes, lanes)
    tile = 64

    def part(index, carry):
        real_rows = pl.ds(pl.multiple_of(index * tile, tile), tile)
        imag_rows = pl.ds(pl.multiple_of(block + index * tile, tile), tile)

        def add(k, total):
            real, imag = total
            tap_r, tap_i = taps_ref[k, real_rows, :], taps_ref[k, imag_rows, :]
            val_r = series_ref[piece + step * k, real_rows, lane]
            val_i = series_ref[piece + step * k, imag_rows, lane]
            if conjugate:
                return (
                    real + tap_r * val_r + tap_i * val_i,
                    imag + tap_r * val_i - tap_i * val_r,
                )
            return real + tap_r * val_r - tap_i * val_i, imag + tap_r * val_i + tap_i * val_r

        zero = jnp.zeros((tile, lanes), F32)
        real, imag = lax.fori_loop(0, count, add, (zero, zero))
        into_ref[real_rows, lane] = real
        into_ref[imag_rows, lane] = imag
        return carry

    lax.fori_loop(0, block // tile, part, 0)


def long_forward_kernel(
    table_ref, series_ref, taps_ref, skip_ref, ah_ref, al_ref, bh_ref, bl_ref, out_ref, spec, work
):
    blocks, rows, block, lanes = series_ref.shape
    piece_spectra(table_ref, series_ref, ah_ref, al_ref, spec)
    for piece in range(spec.shape[0]):
        for row in range(rows):
            couple(table_ref[3, row, piece], -1, taps_ref, spec, piece, row, work, False)
        result = wide_dot(bh_ref[...], bl_ref[...], work[...])
        for row in range(rows):
            at, inside = piece_mask(table_ref, row, piece, block, lanes)
            direct = skip_ref[...] * series_ref[at, row].astype(F32)
            value = result[:, row * lanes : (row + 1) * lanes] + direct
            kept = out_ref[at, row].astype(F32)
            out_ref[at, row] = jnp.where(inside, value, kept).astype(BF16)


def long_forward(table, series, taps_spec, skip, tables):
    blocks, rows, block, lanes = series.shape
    pieces = table.shape[2]
    smem = pl.BlockSpec(memory_space=pltpu.SMEM)
    vmem = pl.BlockSpec(memory_space=pltpu.VMEM)
    return pl.pallas_call(
        long_forward_kernel,
        in_specs=[smem] + [vmem] * 7,
        out_specs=vmem,
        out_shape=jax.ShapeDtypeStruct(series.shape, BF16),
        scratch_shapes=[
            pltpu.VMEM((pieces, 2 * block, rows * lanes), F32),
            pltpu.VMEM((2 * block, rows * lanes), F32),
        ],
        compiler_params=pltpu.CompilerParams(vmem_limit_bytes=VMEM_LIMIT),
        name="long_forward",
    )(table, series, taps_spec, skip, *tables)


def long_backward_kernel(
    table_ref,
    grad_ref,
    series_ref,
    taps_ref,
    skip_ref,
    ah_ref,
    al_ref,
    bh_ref,
    bl_ref,
    out_ref,
    taps_out_ref,
    skip_out_ref,
    spec,
    grad_spec,
    work,
    cross,
):
    blocks, rows, block, lanes = series_ref.shape
    pieces = spec.shape[0]
    piece_spectra(table_ref, grad_ref, ah_ref, al_ref, grad_spec)
    piece_spectra(table_ref, series_ref, ah_ref, al_ref, spec)
    for piece in range(pieces):
        for row in range(rows):
            couple(table_ref[4, row, piece], 1, taps_ref, grad_spec, piece, row, work, True)
        result = wide_dot(bh_ref[...], bl_ref[...], work[...])
        for row in range(rows):
            at, inside = piece_mask(table_ref, row, piece, block, lanes)
            direct = skip_ref[...] * grad_ref[at, row].astype(F32)
            value = result[:, row * lanes : (row + 1) * lanes] + direct
            kept = out_ref[at, row].astype(F32)
            out_ref[at, row] = jnp.where(inside, value, kept).astype(BF16)

    tile = 64
    for k in range(blocks):

        def part(index, carry, k=k):
            real_rows = pl.ds(pl.multiple_of(index * tile, tile), tile)
            imag_rows = pl.ds(pl.multiple_of(block + index * tile, tile), tile)
            total = (jnp.zeros((tile, lanes), F32), jnp.zeros((tile, lanes), F32))
            for row in range(rows):
                lane = pl.ds(row * lanes, lanes)

                def add(piece, total, row=row, lane=lane):
                    real, imag = total
                    weight = jnp.where(table_ref[3, row, piece] > k, 1.0, 0.0)
                    val_r = spec[piece - k, real_rows, lane]
                    val_i = spec[piece - k, imag_rows, lane]
                    out_r = grad_spec[piece, real_rows, lane] * weight
                    out_i = grad_spec[piece, imag_rows, lane] * weight
                    return (
                        real + val_r * out_r + val_i * out_i,
                        imag + val_r * out_i - val_i * out_r,
                    )

                total = lax.fori_loop(k, pieces, add, total)
            cross[k, real_rows, :] = total[0]
            cross[k, imag_rows, :] = total[1]
            return carry

        lax.fori_loop(0, block // tile, part, 0)
    sign = alternating(block, lanes)
    for k in range(blocks):
        if k + 1 < blocks:
            cross[k, :block] = cross[k, :block] + sign * cross[k + 1, block:]
            cross[k, block:] = cross[k, block:] - sign * cross[k + 1, :block]
        taps_out_ref[k] = wide_dot(bh_ref[...], bl_ref[...], cross[k])
    total = jnp.zeros((8, lanes), F32)
    for at in range(blocks):
        for row in range(rows):
            both = grad_ref[at, row].astype(F32) * series_ref[at, row].astype(F32)
            total = total + jnp.sum(both.reshape(block // 8, 8, lanes), axis=0)
    skip_out_ref[...] = jnp.sum(total, axis=0, keepdims=True)


def long_backward(table, grad, series, taps_spec, skip, tables):
    blocks, rows, block, lanes = series.shape
    pieces = table.shape[2]
    smem = pl.BlockSpec(memory_space=pltpu.SMEM)
    vmem = pl.BlockSpec(memory_space=pltpu.VMEM)
    return pl.pallas_call(
        long_backward_kernel,
        in_specs=[smem] + [vmem] * 8,
        out_specs=[vmem] * 3,
        out_shape=[
            jax.ShapeDtypeStruct(series.shape, BF16),
            jax.ShapeDtypeStruct((blocks, block, lanes), F32),
            jax.ShapeDtypeStruct((1, lanes), F32),
        ],
        scratch_shapes=[
            pltpu.VMEM((pieces, 2 * block, rows * lanes), F32),
            pltpu.VMEM((pieces, 2 * block, rows * lanes), F32),
            pltpu.VMEM((2 * block, rows * lanes), F32),
            pltpu.VMEM((blocks, 2 * block, lanes), F32),
        ],
        compiler_params=pltpu.CompilerParams(vmem_limit_bytes=VMEM_LIMIT),
        name="long_backward",
    )(table, grad, series, taps_spec, skip, *tables)


def document_masks(bounds, positions, length):
    lower = jnp.concatenate([jnp.zeros_like(bounds[:, :1]), bounds], axis=1)
    upper = jnp.concatenate([bounds, jnp.full_like(bounds[:, :1], length)], axis=1)
    inside = (positions[None, None, :] >= lower[:, :, None]) & (
        positions[None, None, :] < upper[:, :, None]
    )
    return inside.astype(F32)


def cos_sin(count_a, count_b, modulus):
    table = (
        jnp.arange(count_a, dtype=jnp.int32)[:, None]
        * jnp.arange(count_b, dtype=jnp.int32)[None, :]
        % modulus
    )
    angles = table.astype(F32) * (2.0 * math.pi / modulus)
    return (jnp.cos(angles), jnp.sin(angles))


def make_plan(blocks, block_len):
    outer = 2 * blocks
    cos_outer, sin_outer = cos_sin(outer, outer, outer)
    cos_twist, sin_twist = cos_sin(outer, block_len, outer * block_len)
    cos_inner, sin_inner = cos_sin(block_len, block_len, block_len)
    return (blocks, block_len, cos_outer, sin_outer, cos_twist, sin_twist, cos_inner, sin_inner)


def right_mul(left, table):
    return jnp.einsum("...km,mj->...kj", left, table, precision=HIGH)


def spectrum(series, plan):
    blocks, block_len, cos_outer, sin_outer, cos_twist, sin_twist, cos_inner, sin_inner = plan
    folded = series.reshape(series.shape[:-1] + (blocks, block_len))
    real_a = jnp.einsum("kn,...nm->...km", cos_outer[:, :blocks], folded, precision=HIGH)
    imag_a = -jnp.einsum("kn,...nm->...km", sin_outer[:, :blocks], folded, precision=HIGH)
    real_t = real_a * cos_twist + imag_a * sin_twist
    imag_t = imag_a * cos_twist - real_a * sin_twist
    real_x = right_mul(real_t, cos_inner) + right_mul(imag_t, sin_inner)
    imag_x = right_mul(imag_t, cos_inner) - right_mul(real_t, sin_inner)
    return (real_x, imag_x)


def inverse(real_x, imag_x, plan):
    blocks, block_len, cos_outer, sin_outer, cos_twist, sin_twist, cos_inner, sin_inner = plan
    real_b = right_mul(real_x, cos_inner) - right_mul(imag_x, sin_inner)
    imag_b = right_mul(imag_x, cos_inner) + right_mul(real_x, sin_inner)
    real_u = real_b * cos_twist - imag_b * sin_twist
    imag_u = imag_b * cos_twist + real_b * sin_twist
    folded = jnp.einsum("nk,...km->...nm", cos_outer[:blocks], real_u, precision=HIGH) - jnp.einsum(
        "nk,...km->...nm", sin_outer[:blocks], imag_u, precision=HIGH
    )
    folded = folded * (1.0 / (2 * blocks * block_len))
    return folded.reshape(folded.shape[:-2] + (blocks * block_len,))


def by_channel(blocked):
    blocks, rows, block, lanes = blocked.shape
    return blocked.astype(F32).transpose(1, 3, 0, 2).reshape(rows, lanes, blocks * block)


def by_block(series, blocks):
    rows, lanes, length = series.shape
    return series.reshape(rows, lanes, blocks, length // blocks).transpose(2, 0, 3, 1).astype(BF16)


class WholeSpectra:
    def __init__(self, bounds, taps, skip):
        blocks, block, lanes = taps.shape
        self.blocks, self.plan = blocks, make_plan(blocks, block)
        length = blocks * block
        everywhere = jnp.arange(length, dtype=jnp.int32)
        self.masks = document_masks(bounds, everywhere, length)[:, :, None, :]
        self.skip = skip[0][None, :, None]
        self.taps_real, self.taps_imag = spectrum(taps.reshape(length, lanes).T, self.plan)

    def forward(self, series):
        carried = by_channel(series)
        self.carried = carried
        real, imag = spectrum(self.masks * carried[:, None], self.plan)
        self.spec = real, imag
        docs = inverse(
            real * self.taps_real - imag * self.taps_imag,
            real * self.taps_imag + imag * self.taps_real,
            self.plan,
        )
        conv = jnp.sum(self.masks * docs, axis=1) + self.skip * carried
        return by_block(conv, self.blocks)

    def backward(self, grad):
        g_long = by_channel(grad)
        spec_real, spec_imag = self.spec
        g_skip = jnp.sum(g_long * self.carried, axis=(0, 2))
        real, imag = spectrum(self.masks * g_long[:, None], self.plan)
        docs = inverse(
            self.taps_real * real + self.taps_imag * imag,
            self.taps_real * imag - self.taps_imag * real,
            self.plan,
        )
        g_carried = jnp.sum(self.masks * docs, axis=1) + self.skip * g_long
        cross_real = jnp.sum(real * spec_real + imag * spec_imag, axis=(0, 1))
        cross_imag = jnp.sum(imag * spec_real - real * spec_imag, axis=(0, 1))
        g_taps = inverse(cross_real, cross_imag, self.plan)
        return by_block(g_carried, self.blocks), g_taps.T, g_skip[None, :]


class BlockSpectra:
    def __init__(self, bounds, taps, skip):
        blocks, block, lanes = taps.shape
        self.tables = transform_tables(block)
        self.table = piece_table(bounds, blocks, block)
        self.skip = skip
        self.taps = taps_spectrum(taps, self.tables)

    def forward(self, series):
        self.series = series
        return long_forward(self.table, series, self.taps, self.skip, self.tables)

    def backward(self, grad):
        g_series, g_taps, g_skip = long_backward(
            self.table, grad, self.series, self.taps, self.skip, self.tables
        )
        return g_series, g_taps.reshape(-1, g_taps.shape[2]), g_skip


def device_index():
    return lax.axis_index("rows") * lax.axis_size("seq") + lax.axis_index("seq")


def device_bits():
    return int(math.log2(lax.axis_size("rows") * lax.axis_size("seq")))


def swapped(value, mask_of):
    count = lax.axis_size("rows") * lax.axis_size("seq")
    return lax.ppermute(value, BOTH, [(one, one ^ mask_of(one)) for one in range(count)])


def pick(array, index, axis):
    return lax.dynamic_index_in_dim(array, index, axis=axis, keepdims=False)


def added(kept, arrived, kind):
    return (kept.astype(F32) + arrived.astype(F32)).astype(kind)


def halved(pieces, bit, axis, kind):
    mine = (device_index() >> bit) & 1
    arrived = swapped(pick(pieces, 1 - mine, axis), lambda one: 1 << bit)
    return added(pick(pieces, mine, axis), arrived, kind)


def quartered(pieces, axis, kind):
    index = device_index()
    core, low, high = index & 1, (index >> 1) & 1, (index >> 2) & 1

    def two(low_bit, high_bit):
        return jnp.stack(
            [
                pick(pieces, jnp.where(core == 0, 2 * j + low_bit, 2 * high_bit + j), axis)
                for j in range(2)
            ],
            axis=axis,
        )

    arrived = swapped(two(1 - low, 1 - high), lambda one: 4 if one & 1 else 2)
    pieces = added(two(low, high), arrived, kind)
    mine = jnp.where(core == 0, high, low)
    arrived = swapped(pick(pieces, 1 - mine, axis), lambda one: 2 if one & 1 else 4)
    return added(pick(pieces, mine, axis), arrived, kind)


def scattered(pieces, kind):
    rest = pieces.shape[1:]
    bits = device_bits()
    pieces = quartered(pieces.reshape((-1, 4) + rest), 1, kind)
    for bit in range(3, bits):
        last = bit == bits - 1
        pieces = halved(pieces.reshape((-1, 2) + rest), bit, 1, F32 if last else kind)
    return pieces.reshape(rest)


def weight_gradient(first, second):
    tokens, width = first.shape
    shares = 1 << device_bits()
    share = width // shares
    core = device_index() & 1
    halves = first.reshape(tokens, shares // 2, 2, share).transpose(2, 0, 1, 3)
    halves = halves.reshape(2, tokens, width // 2)

    def product(which):
        return jnp.einsum(
            "ti,tj->ij", pick(halves, which, 0), second, preferred_element_type=F32
        )

    arrived = swapped(product(1 - core).astype(BF16), lambda one: 1)
    kept = added(product(core), arrived, BF16)
    return scattered(kept.reshape(shares // 2, share, second.shape[1]), BF16)


def small_scattered(vectors):
    pieces = halved(vectors.reshape(-1, 2, vectors.shape[1]), 0, 1, F32)
    return scattered(pieces, F32)


def summed(value, bits):
    for bit in bits:
        value = value + swapped(value, lambda one, bit=bit: 1 << bit)
    return value


def back_product(grad_low, weight):
    return jnp.einsum("tj,ij->ti", grad_low, weight, preferred_element_type=F32)


def per_device(
    tokens,
    cotangent,
    bounds,
    ln1_gain,
    ln1_bias,
    in_weight,
    in_bias,
    short_weight,
    short_bias,
    f1_weight,
    f1_bias,
    f2_weight,
    f2_bias,
    f3_weight,
    filter_skip,
    out_weight,
    out_bias,
    ln2_gain,
    ln2_bias,
    up_weight,
    up_bias,
    down_weight,
    down_bias,
):
    seq_count = lax.axis_size("seq")
    row_count, tok_count, width = tokens.shape
    flat_count = row_count * tok_count
    length = tok_count * seq_count
    lanes = f3_weight.shape[1]
    first_channel = lax.axis_index("seq") * lanes
    x_in = tokens.astype(F32).reshape(flat_count, width)
    n1, ln1_pull = jax.vjp(layer_norm, x_in, ln1_gain.astype(F32), ln1_bias.astype(F32))
    n1_low = n1.astype(BF16)
    proj = jnp.dot(n1_low, in_weight, preferred_element_type=F32) + in_bias.astype(F32)
    proj_low = proj.astype(BF16).reshape(row_count, tok_count, 3 * width)
    here = lax.axis_index("seq") * tok_count + jnp.arange(tok_count, dtype=jnp.int32)
    starts = jnp.max(
        jnp.where(bounds[:, :, None] <= here[None, None, :], bounds[:, :, None], 0), axis=1
    )
    keep_one = (here[None, :] - 1 >= starts).astype(F32)[:, :, None]
    keep_two = (here[None, :] - 2 >= starts).astype(F32)[:, :, None]
    rim = passed_along(proj_low[:, tok_count - 2 :, :], "seq", 1)
    extended = jnp.concatenate([rim, proj_low], axis=1).astype(F32)
    current = extended[:, 2:, :]
    before_one = extended[:, 1:-1, :]
    before_two = extended[:, :-2, :]
    taps_short = short_weight.astype(F32)
    shorted = (
        taps_short[0] * current
        + keep_one * taps_short[1] * before_one
        + keep_two * taps_short[2] * before_two
        + short_bias.astype(F32)
    )
    gate_out = shorted[:, :, :width]
    gate_in = shorted[:, :, width : 2 * width]
    values = shorted[:, :, 2 * width :]
    carried_low = (gate_in * values).astype(BF16)

    def to_channels(array):
        array = array.reshape(row_count, tok_count, seq_count, lanes).transpose(2, 0, 1, 3)
        return lax.all_to_all(array, "seq", split_axis=0, concat_axis=0, tiled=True)

    def to_positions(array):
        array = lax.all_to_all(array, "seq", split_axis=0, concat_axis=0, tiled=True)
        return array.transpose(1, 2, 0, 3).reshape(row_count, tok_count, width)

    carried = to_channels(carried_low)

    def make_taps(w_one, b_one, w_two, b_two, w_three):
        return filter_taps(w_one, b_one, w_two, b_two, w_three, first_channel, length)

    taps, filter_pull = jax.vjp(
        make_taps,
        f1_weight.astype(F32),
        f1_bias.astype(F32),
        f2_weight.astype(F32),
        f2_bias.astype(F32),
        f3_weight.astype(F32),
    )
    long_filter = (BlockSpectra if lanes % 128 == 0 else WholeSpectra)(
        bounds, taps.reshape(seq_count, tok_count, lanes), filter_skip.astype(F32)[None, :]
    )
    long_low = long_filter.forward(carried)
    long_seq = to_positions(long_low).astype(F32)
    mixed_low = (gate_out * long_seq).astype(BF16).reshape(flat_count, width)
    branch = jnp.dot(mixed_low, out_weight, preferred_element_type=F32) + out_bias.astype(F32)
    resid = x_in + branch
    n2, ln2_pull = jax.vjp(layer_norm, resid, ln2_gain.astype(F32), ln2_bias.astype(F32))
    n2_low = n2.astype(BF16)
    pre = jnp.dot(n2_low, up_weight, preferred_element_type=F32) + up_bias.astype(F32)
    act, gelu_pull = jax.vjp(gelu_tanh, pre)
    act_low = act.astype(BF16)
    result = (
        resid
        + jnp.dot(act_low, down_weight, preferred_element_type=F32)
        + down_bias.astype(F32)
    )
    output = result.astype(BF16).reshape(row_count, tok_count, width)
    grad_low = cotangent.reshape(flat_count, width)
    grad_float = grad_low.astype(F32)
    g_down_w = weight_gradient(act_low, grad_low)
    g_down_b = jnp.sum(grad_float, axis=0)
    g_act = back_product(grad_low, down_weight)
    (g_pre,) = gelu_pull(g_act)
    g_pre_low = g_pre.astype(BF16)
    g_up_w = weight_gradient(n2_low, g_pre_low)
    g_up_b = jnp.sum(g_pre_low.astype(F32), axis=0)
    g_n2 = back_product(g_pre_low, up_weight)
    g_resid_part, g_ln2_gain, g_ln2_bias = ln2_pull(g_n2)
    g_resid = grad_float + g_resid_part
    g_branch_low = g_resid.astype(BF16)
    g_out_w = weight_gradient(mixed_low, g_branch_low)
    g_out_b = jnp.sum(g_branch_low.astype(F32), axis=0)
    g_mixed = back_product(g_branch_low, out_weight).reshape(row_count, tok_count, width)
    g_gate_out = g_mixed * long_seq
    g_long_low = (g_mixed * gate_out).astype(BF16)
    g_carried_low, g_taps, g_skip = long_filter.backward(to_channels(g_long_low))
    g_f1_w, g_f1_b, g_f2_w, g_f2_b, g_f3_w = filter_pull(g_taps)
    g_carried_seq = to_positions(g_carried_low).astype(F32)
    g_shorted = jnp.concatenate(
        [g_gate_out, g_carried_seq * values, g_carried_seq * gate_in], axis=-1
    )
    lead_one = keep_one * g_shorted
    lead_two = keep_two * g_shorted
    ahead = passed_along(
        jnp.concatenate([lead_one[:, :2], lead_two[:, :2]], axis=1).astype(BF16), "seq", -1
    ).astype(F32)
    after_one = jnp.concatenate([lead_one[:, 1:], ahead[:, :1]], axis=1)
    after_two = jnp.concatenate([lead_two[:, 2:], ahead[:, 2:4]], axis=1)
    g_proj = taps_short[0] * g_shorted + taps_short[1] * after_one + taps_short[2] * after_two
    g_short_w = jnp.stack(
        [
            jnp.sum(g_shorted * current, axis=(0, 1)),
            jnp.sum(lead_one * before_one, axis=(0, 1)),
            jnp.sum(lead_two * before_two, axis=(0, 1)),
        ],
        axis=0,
    )
    g_short_b = jnp.sum(g_shorted, axis=(0, 1))
    g_proj_low = g_proj.astype(BF16).reshape(flat_count, 3 * width)
    g_in_w = weight_gradient(n1_low, g_proj_low)
    g_in_b = jnp.sum(g_proj_low.astype(F32), axis=0)
    g_n1 = back_product(g_proj_low, in_weight)
    g_x_part, g_ln1_gain, g_ln1_bias = ln1_pull(g_n1)
    grad_tokens = (g_resid + g_x_part).reshape(row_count, tok_count, width)

    def lined(parts):
        flat = jnp.concatenate([part.reshape(-1) for part in parts])
        return jnp.pad(flat, (0, -flat.shape[0] % 128)).reshape(-1, 128)

    net = lined((g_f1_w, g_f1_b, g_f2_w, g_f2_b))
    net_rows = net.shape[0]
    own = lined((g_f3_w, g_skip))
    bits = device_bits()
    seq_bits = int(math.log2(seq_count))
    joint = summed(jnp.concatenate([net, own]), range(seq_bits, bits))
    net = summed(joint[:net_rows], range(seq_bits)).reshape(-1)
    own = joint[net_rows:].reshape(-1)
    g_f1_w, g_f1_b, g_f2_w, g_f2_b = (
        part.reshape(like.shape)
        for part, like in zip(
            jnp.split(net, np.cumsum([f1_weight.size, f1_bias.size, f2_weight.size, f2_bias.size])),
            (f1_weight, f1_bias, f2_weight, f2_bias),
        )
    )
    g_f3_w = own[: f3_weight.size].reshape(f3_weight.shape)
    g_skip = own[f3_weight.size : f3_weight.size + lanes]

    shares = 1 << bits
    vectors = (g_ln2_gain, g_ln2_bias, g_up_b, g_down_b, g_out_b)
    vectors += (g_ln1_gain, g_ln1_bias, g_in_b, g_short_b) + tuple(g_short_w)
    rows = jnp.concatenate([v.reshape(shares, -1) for v in vectors], axis=1)
    sums = small_scattered(rows)
    cuts = np.cumsum([v.shape[0] // shares for v in vectors])[:-1]
    (
        g_ln2_gain,
        g_ln2_bias,
        g_up_b,
        g_down_b,
        g_out_b,
        g_ln1_gain,
        g_ln1_bias,
        g_in_b,
        g_short_b,
        *g_short_w,
    ) = jnp.split(sums, cuts)
    return (
        output,
        grad_tokens,
        g_ln1_gain,
        g_ln1_bias,
        g_in_w,
        g_in_b,
        jnp.stack(g_short_w),
        g_short_b,
        g_f1_w,
        g_f1_b,
        g_f2_w,
        g_f2_b,
        g_f3_w,
        g_skip,
        g_out_w,
        g_out_b,
        g_ln2_gain,
        g_ln2_bias,
        g_up_w,
        g_up_b,
        g_down_w,
        g_down_b,
    )


def solution(mesh):
    return jax.shard_map(
        per_device,
        mesh=mesh,
        in_specs=(
            P("rows", "seq", None),
            P("rows", "seq", None),
            P("rows", None),
            P(),
            P(),
            P(),
            P(),
            P(),
            P(),
            P(),
            P(),
            P(),
            P(),
            P(None, "seq"),
            P("seq"),
            P(),
            P(),
            P(),
            P(),
            P(),
            P(),
            P(),
            P(),
        ),
        out_specs=(
            P("rows", "seq", None),
            P("rows", "seq", None),
            P(("rows", "seq")),
            P(("rows", "seq")),
            P(("rows", "seq"), None),
            P(("rows", "seq")),
            P(None, ("rows", "seq")),
            P(("rows", "seq")),
            P(),
            P(),
            P(),
            P(),
            P(None, "seq"),
            P("seq"),
            P(("rows", "seq"), None),
            P(("rows", "seq")),
            P(("rows", "seq")),
            P(("rows", "seq")),
            P(("rows", "seq"), None),
            P(("rows", "seq")),
            P(("rows", "seq"), None),
            P(("rows", "seq")),
        ),
        check_vma=False,
    )
```

time: 1790 us -> 624 us (0.35)
  waiting for transfers between devices: 797 us -> 150 us
  matrix products: 699 us -> 117 us
  Pallas kernels: 0 us -> 49.9 us
  starting transfers between devices: 21.7 us -> 57.7 us
  blocking collectives: 20.4 us -> 0 us
    reduce_scatter x4 -> x0, waiting for transfers between devices: 663 us -> none  [the longest x1 187 us: per_device(): lax.psum_scatter(g_up_w, ('rows', 'seq'), scatter_dimension=0, tiled=True)]
    dot_general x48 -> x16, matrix products: 680 us -> 98.9 us  [the longest x8 36.4 us: product(): jnp.einsum('ti,tj->ij', pick(halves, which, 0), second, preferred_element...]
    ppermute x0 -> x30, waiting for transfers between devices: none -> 124 us  [swapped(): lax.ppermute(value, BOTH, [(one, one ^ mask_of(one)) for one in range(cou...]
    unnamed x8 -> x0, waiting for transfers between devices: 99.4 us -> none
    pallas_call x0 -> x3, Pallas kernels: none -> 49.9 us  [the longest x1 29.4 us: long_backward(): pl.pallas_call(long_backward_kernel, in_specs=[smem] + [vmem] * 8, out_sp...]
    ppermute x0 -> x30, starting transfers between devices: none -> 35.5 us  [swapped(): lax.ppermute(value, BOTH, [(one, one ^ mask_of(one)) for one in range(cou...]
    reshape x2 -> x12, local copies, waits for them, and re-layouts: 6.35 us -> 31.8 us  [the longest x2 18.8 us: weight_gradient(): halves = first.reshape(tokens, shares // 2, 2, share).transpose(2, 0, 1, 3)]
    unnamed x236 -> x166, local copies, waits for them, and re-layouts: 31.7 us -> 11.1 us
  transfers between devices with their start and end apart: 12 -> 36, of which waited for: 9 -> 16; matrix products, arithmetic and copies ran while one was open for 11% -> 41% of each run, Pallas kernels for 0% -> 6%
where the time goes in v1:
time: 624 us; the launch traced here: 614 us
  waiting for transfers between devices  150 us (24%)
  local copies, waits for them, and re-layouts  134 us (21%)
  matrix products  117 us (19%)
  other arithmetic  103 us (17%)
  starting transfers between devices  57.7 us (9%)
  Pallas kernels  49.9 us (8%)
    ppermute x30, waiting for transfers between devices, swapped(): lax.ppermute(value, BOTH, [(one, one ^ mask_of(one)) for one in range(cou...  124 us
    dot_general x8, matrix products, product(): jnp.einsum('ti,tj->ij', pick(halves, which, 0), second, preferred_element...  36.4 us
    ppermute x30, starting transfers between devices, swapped(): lax.ppermute(value, BOTH, [(one, one ^ mask_of(one)) for one in range(cou...  35.5 us
    dot_general x4, matrix products, back_product(): return jnp.einsum('tj,ij->ti', grad_low, weight, preferred_element_type=F32)  34.1 us
    pallas_call x1, Pallas kernels, long_backward(): pl.pallas_call(long_backward_kernel, in_specs=[smem] + [vmem] * 8, out_sp...  29.4 us
    reduce_sum x1, other arithmetic, per_device(): jnp.sum(lead_two * before_two, axis=(0, 1))  19.3 us
    reshape x2, local copies, waits for them, and re-layouts, weight_gradient(): halves = first.reshape(tokens, shares // 2, 2, share).transpose(2, 0, 1, 3)  18.8 us
    reduce_sum x1, other arithmetic, per_device(): g_in_b = jnp.sum(g_proj_low.astype(F32), axis=0)  16.8 us
  transfers between devices with their start and end apart: 36, of which 16 were waited for; matrix products, arithmetic and copies ran while one was open for 41% of the time, Pallas kernels for 6%

profile of v1, /device:TPU:0, one launch (start us, length us, event | category | flops | bytes accessed | tf_op | source)
XLA Modules:
  0.0 613.8 jit_solution(15780335480403407314)
XLA Ops:
  7.8 6.4 %add_convert_fusion.4 = bf16[512,3072]{1,0:T(8,128)(2,1)S(1)} fusion(bf16[512,1024]{1,0:T(8,128)(2,1)S(1)} %add_convert_fusion.12, bf16[1024,3072]{1,0:T(8,128)(2,1)} %param.34, f32[3072]{0:T(1024)S(1)} %convert_element_type.372), kind=kOutput, calls=%fused_computation.29 | convolution fusion | flops 3224371200 | bytes 10498048 | tf_op jit(solution)/shard_map/dot_general | solution.py:573
  28.5 4.7 copy.206
  39.2 5.5 add_add_fusion
  48.6 5.5 all-to-all-start
  59.2 10.3 %all-to-all-done.series_ref = bf16[8,2,256,128]{3,2,1,0:T(8,128)(2,1)S(1)} async-done(((bf16[8,2,256,128]{3,2,1,0:T(8,128)(2,1)}), bf16[8,2,256,128]{3,2,1,0:T(8,128)(2,1)S(1)}, u32[]{:S(2)}, u32[]{:S(2)}) %all-to-all-start) | async-done | bytes 1048608 | tf_op jit(solution)/shard_map/all_to_all | solution.py:600
  70.4 16.0 %long_forward.1 = bf16[8,2,256,128]{3,2,1,0:T(8,128)(2,1)} custom-call(s32[5,2,10]{2,1,0:T(2,128)} %copy-done.52, bf16[8,2,256,128]{3,2,1,0:T(8,128)(2,1)} %copy-done.14, f32[8,512,128]{2,1,0:T(8,128)} %taps_spectrum.1.taps_ref, f32[1,128]{1,0:T(1,128)} %bitcast_convert_fusion.skip_ref, bf16[512,256]{1,0:T(8,128)(2,1)} %constant.287.clone.high_ref.ah_ref, ...), custom_call_target="tpu_custom_call" | custom-call | tf_op jit(solution)/shard_map/long_forward/pallas_call | solution.py:210
  90.7 15.3 %all-to-all-done.1 = bf16[8,2,256,128]{3,2,1,0:T(8,128)(2,1)S(1)} async-done(((bf16[8,2,256,128]{3,2,1,0:T(8,128)(2,1)}), bf16[8,2,256,128]{3,2,1,0:T(8,128)(2,1)S(1)}, u32[]{:S(2)}, u32[]{:S(2)}) %all-to-all-start.1) | async-done | bytes 1048608 | tf_op jit(solution)/shard_map/all_to_all | solution.py:603
  123.5 10.5 %fusion.80 = f32[512,4096]{1,0:T(8,128)} fusion(bf16[512,1024]{1,0:T(8,128)(2,1)S(1)} %add_convert_fusion.11, bf16[1024,4096]{1,0:T(8,128)(2,1)} %param.48), kind=kOutput, calls=%fused_computation.259 | convolution fusion | flops 4294967296 | bytes 17825792 | tf_op jit(solution)/shard_map/dot_general | solution.py:629
  134.0 17.6 %convert_reduce_fusion = (f32[4096]{0:T(1024)}, bf16[512,4096]{1,0:T(8,128)(2,1)}, bf16[512,4096]{1,0:T(8,128)(2,1)}) fusion(f32[512,4096]{1,0:T(8,128)} %fusion.80, f32[4096]{0:T(1024)S(1)} %convert_element_type.390, bf16[512,1024]{1,0:T(8,128)(2,1)S(1)} %bitcast.305, bf16[4096,1024]{1,0:T(8,128)(2,1)} %param.50), kind=kOutput, calls=%fused_computation.11 | convolution fusion | flops 4347392000 | bytes 26247168 | tf_op jit(solution)/shard_map/tj,ij->ti/dot_general | solution.py:536
  151.6 7.2 %multiply_reduce_fusion.4 = (f32[1024]{0:T(1024)S(1)}, f32[512]{0:T(512)S(1)}, f32[1024]{0:T(1024)S(1)}, f32[512,1024]{1,0:T(8,128)S(1)}) fusion(f32[512,1024]{1,0:T(8,128)S(1)} %get-tuple-element.115, f32[512]{0:T(512)S(1)} %fusion.62, f32[512]{0:T(512)S(1)} %broadcast_multiply_fusion.2, f32[1024]{0:T(1024)S(1)} %convert_element_type.387, ...), kind=kOutput, calls=%fused_computation.74 | convolution fusion | flops 4299159040 | bytes 16795648 | tf_op jit(solution)/shard_map/tj,ij->ti/dot_general | solution.py:536
  193.0 7.7 %reshape.699 = bf16[512,16,2,128]{3,2,1,0:T(2,128)(2,1)} reshape(bf16[512,4096]{1,0:T(8,128)(2,1)} %get-tuple-element.59) | data formatting | bytes 8388608 | tf_op jit(solution)/shard_map/reshape | solution.py:511
  200.7 11.1 %copy.242 = bf16[512,16,2,128]{0,3,1,2:T(8,128)(2,1)} copy(bf16[512,16,2,128]{3,2,1,0:T(2,128)(2,1)} %reshape.699) | data formatting | bytes 8388608 | tf_op jit(solution)/shard_map/reshape | solution.py:511
  217.8 29.4 %long_backward.1 = (bf16[8,2,256,128]{3,2,1,0:T(8,128)(2,1)}, f32[8,256,128]{2,1,0:T(8,128)}, f32[1,128]{1,0:T(1,128)}) custom-call(s32[5,2,10]{2,1,0:T(2,128)} %copy-done.52, bf16[8,2,256,128]{3,2,1,0:T(8,128)(2,1)} %all-to-all-done.2.grad_ref, bf16[8,2,256,128]{3,2,1,0:T(8,128)(2,1)} %copy-done.14, f32[8,512,128]{2,1,0:T(8,128)} %taps_spectrum.1.taps_ref, ...), custom_call_target="tpu_custom_call" | custom-call | tf_op jit(solution)/shard_map/long_backward/pallas_call | solution.py:304
  260.9 6.0 convolution_convert_fusion.2
  269.6 6.5 %convolution_convert_fusion = bf16[512,4096]{1,0:T(8,128)(2,1)} fusion(bf16[512,4096]{1,0:T(8,128)(2,1)} %get-tuple-element.52, bf16[2,512,512]{1,2,0:T(8,128)(2,1)S(1)} %bitcast.336, s32[]{:T(128)S(6)} %select_n.202), kind=kOutput, calls=%fused_computation.30 | convolution fusion | flops 2149580800 | bytes 8912900 | tf_op jit(solution)/shard_map/ti,tj->ij/dot_general | solution.py:515
  287.8 8.9 %add_convert_fusion.10 = bf16[512,1024]{1,0:T(8,128)(2,1)} fusion(f32[512,1024]{1,0:T(8,128)S(1)} %copy-done.8, bf16[512,4096]{1,0:T(8,128)(2,1)S(1)} %copy-done.23, bf16[4096,1024]{1,0:T(8,128)(2,1)} %param.50, f32[1024]{0:T(1024)S(1)} %copy-done.64), kind=kOutput, calls=%fused_computation.80 | convolution fusion | flops 4296540160 | bytes 15732736 | tf_op jit(solution)/shard_map/dot_general | solution.py:634
  318.9 19.3 %multiply_reduce_fusion = (f32[3072]{0:T(1024)S(1)}, f32[3072]{0:T(1024)}, f32[3072]{0:T(1024)}, f32[3072]{0:T(1024)}, f32[2,256,3072]{1,2,0:T(8,128)}, /*index=5*/f32[2,256,3072]{1,2,0:T(8,128)}) fusion(f32[2,258,3072]{1,2,0:T(8,128)} %copy-done.2, f32[2,256,1024]{1,2,0:T(8,128)} %get-tuple-element.61, f32[2,256,1024]{1,2,0:T(8,128)S(1)} %get-tuple-element.60, ...), kind=kLoop, calls=%fused_computation.23 | loop fusion | flops 17289216 | bytes 37801984 | tf_op jit(solution)/shard_map/reduce_sum | solution.py:674
  352.1 7.5 %slice.125 = f32[2,255,3072]{1,2,0:T(8,128)} slice(f32[2,256,3072]{1,2,0:T(8,128)} %get-tuple-element.43), slice={[0:2], [1:256], [0:3072]} | slice | bytes 12533760 | tf_op jit(solution)/shard_map/slice | solution.py:667
  376.2 16.8 %convert_reduce_fusion.1 = (f32[3072]{0:T(1024)S(1)}, bf16[2,256,3072]{1,2,0:T(8,128)(2,1)}, f32[2,256,3072]{1,2,0:T(8,128)}, f32[2,256,3072]{1,2,0:T(8,128)}) fusion(f32[3072]{0:T(1024)S(1)} %bitcast.350, f32[3072]{0:T(1024)S(1)} %bitcast.347, f32[2,256,1024]{1,2,0:T(8,128)} %get-tuple-element.61, f32[2,256,1024]{1,2,0:T(8,128)S(1)} %get-tuple-element.60, ...), kind=kLoop, calls=%fused_computation.26 | loop fusion | flops 18871296 | bytes 34652160 | tf_op jit(solution)/shard_map/reduce_sum | solution.py:681
  392.9 6.6 %copy.220 = f32[2,256,3072]{2,1,0:T(8,128)} copy(f32[2,256,3072]{1,2,0:T(8,128)} %get-tuple-element.47) | data formatting | bytes 12582912 | tf_op jit(solution)/shard_map/concatenate | solution.py:667
  399.5 6.8 %copy.222 = f32[2,256,3072]{2,1,0:T(8,128)} copy(f32[2,256,3072]{1,2,0:T(8,128)} %get-tuple-element.48) | data formatting | bytes 12582912 | tf_op jit(solution)/shard_map/concatenate | solution.py:668
  406.3 6.9 %fusion.9 = bf16[512,3072]{1,0:T(8,128)(2,1)S(1)} fusion(f32[512,1024]{1,0:T(8,128)} %bitcast.308, f32[512,1024]{1,0:T(8,128)S(1)} %bitcast.307, f32[512,1024]{1,0:T(8,128)} %get-tuple-element.117, f32[2,256,3072]{2,1,0:T(8,128)} %copy.222, f32[2,256,3072]{2,1,0:T(8,128)} %copy.220, f32[3072]{0:T(1024)S(1)} %bitcast.351, f32[3072]{0:T(1024)S(1)} %bitcast.348, ...), kind=kLoop, calls=%fused_computation.16 | loop fusion | flops 12582912 | bytes 22056960 | tf_op jit(solution)/shard_map/convert_element_type | solution.py:679
  413.3 5.8 fusion.69
  425.7 5.1 copy.225
  430.8 5.7 convolution_convert_fusion.1
  457.3 5.5 add_convert_fusion
  478.2 12.0 %collective-permute-done.28 = bf16[4,2,128,1024]{3,2,0,1:T(8,128)(2,1)S(1)} collective-permute-done((bf16[4,2,128,1024]{3,2,0,1:T(8,128)(2,1)S(1)}, bf16[4,2,128,1024]{3,2,0,1:T(8,128)(2,1)S(1)}, u32[]{:S(2)}, u32[]{:S(2)}) %collective-permute-start.28) | collective-permute-done | bytes 2097184 | tf_op jit(solution)/shard_map/ppermute | solution.py:459
  493.0 31.0 %collective-permute-done.23 = bf16[4,2,32,4096]{3,2,0,1:T(8,128)(2,1)S(1)} collective-permute-done((bf16[4,2,32,4096]{3,2,0,1:T(8,128)(2,1)S(1)}, bf16[4,2,32,4096]{3,2,0,1:T(8,128)(2,1)S(1)}, u32[]{:S(2)}, u32[]{:S(2)}) %collective-permute-start.23) | collective-permute-done | bytes 2097184 | tf_op jit(solution)/shard_map/ppermute | solution.py:459
  526.7 28.9 %collective-permute-done.8 = bf16[4,2,32,3072]{3,2,0,1:T(8,128)(2,1)S(1)} collective-permute-done((bf16[4,2,32,3072]{3,2,0,1:T(8,128)(2,1)S(1)}, bf16[4,2,32,3072]{3,2,0,1:T(8,128)(2,1)S(1)}, u32[]{:S(2)}, u32[]{:S(2)}) %collective-permute-start.8) | collective-permute-done | bytes 1572896 | tf_op jit(solution)/shard_map/ppermute | solution.py:459
  561.6 7.1 %collective-permute-done.9 = bf16[4,32,3072]{2,1,0:T(8,128)(2,1)S(1)} collective-permute-done((bf16[4,32,3072]{2,1,0:T(8,128)(2,1)S(1)}, bf16[4,32,3072]{2,1,0:T(8,128)(2,1)S(1)}, u32[]{:S(2)}, u32[]{:S(2)}) %collective-permute-start.9) | collective-permute-done | bytes 786464 | tf_op jit(solution)/shard_map/ppermute | solution.py:459
  571.3 16.1 %collective-permute-done.10 = bf16[2,32,3072]{2,1,0:T(8,128)(2,1)S(1)} collective-permute-done((bf16[2,32,3072]{2,1,0:T(8,128)(2,1)S(1)}, bf16[2,32,3072]{2,1,0:T(8,128)(2,1)S(1)}, u32[]{:S(2)}, u32[]{:S(2)}) %collective-permute-start.10) | collective-permute-done | bytes 393248 | tf_op jit(solution)/shard_map/ppermute | solution.py:459
  595.3 11.6 %collective-permute-done.11 = bf16[1,32,3072]{2,1,0:T(8,128)(2,1)S(1)} collective-permute-done((bf16[1,32,3072]{2,1,0:T(8,128)(2,1)S(1)}, bf16[1,32,3072]{2,1,0:T(8,128)(2,1)S(1)}, u32[]{:S(2)}, u32[]{:S(2)}) %collective-permute-start.11) | collective-permute-done | bytes 196640 | tf_op jit(solution)/shard_map/ppermute | solution.py:459
  (413 shorter events, 250.4 us)
Async XLA Ops:
  15.9 17.3 %collective-permute-start = (bf16[2,2,3072]{2,1,0:T(2,128)(2,1)S(1)}, bf16[2,2,3072]{2,1,0:T(2,128)(2,1)S(1)}, u32[]{:S(2)}, u32[]{:S(2)}) collective-permute-start(bf16[2,2,3072]{2,1,0:T(2,128)(2,1)S(1)} %slice.116), channel_id=1, source_target_pairs={{0,1},{1,2},{2,3},{3,4},{4,5},{5,6},{6,7},{8,9},{9,10},{10,11},{11... | collective-permute-start | bytes 73736 | tf_op jit(solution)/shard_map/ppermute | solution.py:28
  48.6 20.8 %all-to-all-start = ((bf16[8,2,256,128]{3,2,1,0:T(8,128)(2,1)}), bf16[8,2,256,128]{3,2,1,0:T(8,128)(2,1)S(1)}, u32[]{:S(2)}, u32[]{:S(2)}) async-start(bf16[8,2,256,128]{3,2,1,0:T(8,128)(2,1)} %bitcast.322), calls=%async_computation | async-start | bytes 2097152 | tf_op jit(solution)/shard_map/all_to_all | solution.py:600
  86.5 19.5 %all-to-all-start.1 = ((bf16[8,2,256,128]{3,2,1,0:T(8,128)(2,1)}), bf16[8,2,256,128]{3,2,1,0:T(8,128)(2,1)S(1)}, u32[]{:S(2)}, u32[]{:S(2)}) async-start(bf16[8,2,256,128]{3,2,1,0:T(8,128)(2,1)} %long_forward.1), calls=%async_computation.1 | async-start | bytes 2097152 | tf_op jit(solution)/shard_map/all_to_all | solution.py:603
  175.6 42.2 %all-to-all-start.2 = ((bf16[8,2,256,128]{3,2,1,0:T(8,128)(2,1)}), bf16[8,2,256,128]{3,2,1,0:T(8,128)(2,1)}, u32[]{:S(2)}, u32[]{:S(2)}) async-start(bf16[8,2,256,128]{3,2,1,0:T(8,128)(2,1)} %bitcast.21), calls=%async_computation.2 | async-start | bytes 2097152 | tf_op jit(solution)/shard_map/all_to_all | solution.py:600
  217.4 63.9 %collective-permute-start.17 = (bf16[512,1024]{1,0:T(8,128)(2,1)}, bf16[512,1024]{1,0:T(8,128)(2,1)}, u32[]{:S(2)}, u32[]{:S(2)}) collective-permute-start(bf16[512,1024]{1,0:T(8,128)(2,1)} %convolution_convert_fusion.3), channel_id=1, source_target_pairs={{0,1},{1,0},{2,3},{3,2},{4,5},{5,4},{6,7},{7,6},{8,9},{9,8},{10,11... | collective-permute-start | bytes 3145736 | tf_op jit(solution)/shard_map/ppermute | solution.py:459
  258.2 9.5 %collective-permute-start.12 = (f32[115,128]{1,0:T(8,128)S(1)}, f32[115,128]{1,0:T(8,128)S(1)}, u32[]{:S(2)}, u32[]{:S(2)}) collective-permute-start(f32[115,128]{1,0:T(8,128)S(1)} %pad_maximum_fusion.7), channel_id=1, source_target_pairs={{0,8},{1,9},{2,10},{3,11},{4,12},{5,13},{6,14},{7,15},{8,0},{9,1},... | collective-permute-start | bytes 176648 | tf_op jit(solution)/shard_map/ppermute | solution.py:459
  267.4 189.9 %collective-permute-start.27 = (bf16[2048,1024]{1,0:T(8,128)(2,1)}, bf16[2048,1024]{1,0:T(8,128)(2,1)}, u32[]{:S(2)}, u32[]{:S(2)}) collective-permute-start(bf16[2048,1024]{1,0:T(8,128)(2,1)} %convolution_convert_fusion.2), channel_id=1, source_target_pairs={{0,1},{1,0},{2,3},{3,2},{4,5},{5,4},{6,7},{7,6},{8,9},{9,8},{10,11... | collective-permute-start | bytes 12582920 | tf_op jit(solution)/shard_map/ppermute | solution.py:459
  267.7 13.1 %collective-permute-start.13 = (f32[115,128]{1,0:T(8,128)S(1)}, f32[115,128]{1,0:T(8,128)S(1)}, u32[]{:S(2)}, u32[]{:S(2)}) collective-permute-start(f32[115,128]{1,0:T(8,128)S(1)} %fusion.123), channel_id=1, source_target_pairs={{0,16},{1,17},{2,18},{3,19},{4,20},{5,21},{6,22},{7,23},{8,24},{9,... | collective-permute-start | bytes 176648 | tf_op jit(solution)/shard_map/ppermute | solution.py:459
  276.1 188.2 %collective-permute-start.22 = (bf16[512,4096]{1,0:T(8,128)(2,1)}, bf16[512,4096]{1,0:T(8,128)(2,1)}, u32[]{:S(2)}, u32[]{:S(2)}) collective-permute-start(bf16[512,4096]{1,0:T(8,128)(2,1)} %convolution_convert_fusion), channel_id=1, source_target_pairs={{0,1},{1,0},{2,3},{3,2},{4,5},{5,4},{6,7},{7,6},{8,9},{9,8},{10,11... | collective-permute-start | bytes 12582920 | tf_op jit(solution)/shard_map/ppermute | solution.py:459
  276.3 34.7 %all-to-all-start.3 = ((bf16[8,2,256,128]{3,2,1,0:T(8,128)(2,1)}), bf16[8,2,256,128]{3,2,1,0:T(8,128)(2,1)}, u32[]{:S(2)}, u32[]{:S(2)}) async-start(bf16[8,2,256,128]{3,2,1,0:T(8,128)(2,1)} %get-tuple-element.25), calls=%async_computation.3 | async-start | bytes 2097152 | tf_op jit(solution)/shard_map/all_to_all | solution.py:603
  280.8 6.4 %collective-permute-start.14 = (f32[50,128]{1,0:T(8,128)S(1)}, f32[50,128]{1,0:T(8,128)S(1)}, u32[]{:S(2)}, u32[]{:S(2)}) collective-permute-start(f32[50,128]{1,0:T(8,128)S(1)} %slice.131), channel_id=1, source_target_pairs={{0,1},{1,0},{2,3},{3,2},{4,5},{5,4},{6,7},{7,6},{8,9},{9,8},{10,11... | collective-permute-start | bytes 76808 | tf_op jit(solution)/shard_map/ppermute | solution.py:459
  285.7 22.5 %collective-permute-start.18 = (bf16[4,2,32,1024]{3,2,0,1:T(8,128)(2,1)}, bf16[4,2,32,1024]{3,2,0,1:T(8,128)(2,1)}, u32[]{:S(2)}, u32[]{:S(2)}) collective-permute-start(bf16[4,2,32,1024]{3,2,0,1:T(8,128)(2,1)} %pad_maximum_fusion.6), channel_id=1, source_target_pairs={{0,2},{1,5},{2,0},{3,7},{4,6},{5,1},{6,4},{7,3},{8,10},{9,13},{10,... | collective-permute-start | bytes 1572872 | tf_op jit(solution)/shard_map/ppermute | solution.py:459
  287.2 14.3 %collective-permute-start.15 = (f32[50,128]{1,0:T(8,128)S(1)}, f32[50,128]{1,0:T(8,128)}, u32[]{:S(2)}, u32[]{:S(2)}) collective-permute-start(f32[50,128]{1,0:T(8,128)S(1)} %slice_add_fusion), channel_id=1, source_target_pairs={{0,2},{1,3},{2,0},{3,1},{4,6},{5,7},{6,4},{7,5},{8,10},{9,11},{10,... | collective-permute-start | bytes 76808 | tf_op jit(solution)/shard_map/ppermute | solution.py:459
  309.5 40.8 %collective-permute-start.19 = (bf16[4,32,1024]{2,1,0:T(8,128)(2,1)S(1)}, bf16[4,32,1024]{2,1,0:T(8,128)(2,1)}, u32[]{:S(2)}, u32[]{:S(2)}) collective-permute-start(bf16[4,32,1024]{2,1,0:T(8,128)(2,1)S(1)} %dynamic-slice_bitcast_fusion.18), channel_id=1, source_target_pairs={{0,4},{1,3},{2,6},{3,1},{4,0},{5,7},{6,2},{7,5},{8,12},{9,11},{10,... | collective-permute-start | bytes 786440 | tf_op jit(solution)/shard_map/ppermute | solution.py:459
  348.8 22.9 %collective-permute-start.1 = (bf16[2,4,3072]{2,1,0:T(4,128)(2,1)}, bf16[2,4,3072]{2,1,0:T(4,128)(2,1)S(1)}, u32[]{:S(2)}, u32[]{:S(2)}) collective-permute-start(bf16[2,4,3072]{2,1,0:T(4,128)(2,1)} %pad_maximum_fusion.8), channel_id=1, source_target_pairs={{1,0},{2,1},{3,2},{4,3},{5,4},{6,5},{7,6},{9,8},{10,9},{11,10},{12... | collective-permute-start | bytes 147464 | tf_op jit(solution)/shard_map/ppermute | solution.py:28
  368.7 80.5 %collective-permute-start.20 = (bf16[2,32,1024]{2,1,0:T(8,128)(2,1)}, bf16[2,32,1024]{2,1,0:T(8,128)(2,1)}, u32[]{:S(2)}, u32[]{:S(2)}) collective-permute-start(bf16[2,32,1024]{2,1,0:T(8,128)(2,1)} %dynamic-slice_bitcast_fusion.23), channel_id=1, source_target_pairs={{0,8},{1,9},{2,10},{3,11},{4,12},{5,13},{6,14},{7,15},{8,0},{9,1},... | collective-permute-start | bytes 393224 | tf_op jit(solution)/shard_map/ppermute | solution.py:459
  424.7 11.8 %collective-permute-start.2 = (f32[16,800]{1,0:T(8,128)S(1)}, f32[16,800]{1,0:T(8,128)S(1)}, u32[]{:S(2)}, u32[]{:S(2)}) collective-permute-start(f32[16,800]{1,0:T(8,128)S(1)} %bitcast.353), channel_id=1, source_target_pairs={{0,1},{1,0},{2,3},{3,2},{4,5},{5,4},{6,7},{7,6},{8,9},{9,8},{10,11... | collective-permute-start | bytes 153608 | tf_op jit(solution)/shard_map/ppermute | solution.py:459
  436.5 36.2 %collective-permute-start.7 = (bf16[512,3072]{1,0:T(8,128)(2,1)}, bf16[512,3072]{1,0:T(8,128)(2,1)}, u32[]{:S(2)}, u32[]{:S(2)}) collective-permute-start(bf16[512,3072]{1,0:T(8,128)(2,1)} %convolution_convert_fusion.1), channel_id=1, source_target_pairs={{0,1},{1,0},{2,3},{3,2},{4,5},{5,4},{6,7},{7,6},{8,9},{9,8},{10,11... | collective-permute-start | bytes 9437192 | tf_op jit(solution)/shard_map/ppermute | solution.py:459
  442.1 5.1 collective-permute-start.4
  452.1 19.9 %collective-permute-start.21 = (bf16[1,32,1024]{2,1,0:T(8,128)(2,1)S(1)}, bf16[1,32,1024]{2,1,0:T(8,128)(2,1)S(1)}, u32[]{:S(2)}, u32[]{:S(2)}) collective-permute-start(bf16[1,32,1024]{2,1,0:T(8,128)(2,1)S(1)} %constant_dynamic-slice_fusion.2), channel_id=1, source_target_pairs={{0,16},{1,17},{2,18},{3,19},{4,20},{5,21},{6,22},{7,23},{8,24},{9,... | collective-permute-start | bytes 196616 | tf_op jit(solution)/shard_map/ppermute | solution.py:459
  463.5 26.7 %collective-permute-start.28 = (bf16[4,2,128,1024]{3,2,0,1:T(8,128)(2,1)S(1)}, bf16[4,2,128,1024]{3,2,0,1:T(8,128)(2,1)S(1)}, u32[]{:S(2)}, u32[]{:S(2)}) collective-permute-start(bf16[4,2,128,1024]{3,2,0,1:T(8,128)(2,1)S(1)} %pad_maximum_fusion.4), channel_id=1, source_target_pairs={{0,2},{1,5},{2,0},{3,7},{4,6},{5,1},{6,4},{7,3},{8,10},{9,13},{10,... | collective-permute-start | bytes 6291464 | tf_op jit(solution)/shard_map/ppermute | solution.py:459
  470.6 53.4 %collective-permute-start.23 = (bf16[4,2,32,4096]{3,2,0,1:T(8,128)(2,1)S(1)}, bf16[4,2,32,4096]{3,2,0,1:T(8,128)(2,1)S(1)}, u32[]{:S(2)}, u32[]{:S(2)}) collective-permute-start(bf16[4,2,32,4096]{3,2,0,1:T(8,128)(2,1)S(1)} %pad_maximum_fusion.3), channel_id=1, source_target_pairs={{0,2},{1,5},{2,0},{3,7},{4,6},{5,1},{6,4},{7,3},{8,10},{9,13},{10,... | collective-permute-start | bytes 6291464 | tf_op jit(solution)/shard_map/ppermute | solution.py:459
  476.8 78.7 %collective-permute-start.8 = (bf16[4,2,32,3072]{3,2,0,1:T(8,128)(2,1)S(1)}, bf16[4,2,32,3072]{3,2,0,1:T(8,128)(2,1)S(1)}, u32[]{:S(2)}, u32[]{:S(2)}) collective-permute-start(bf16[4,2,32,3072]{3,2,0,1:T(8,128)(2,1)S(1)} %pad_maximum_fusion.5), channel_id=1, source_target_pairs={{0,2},{1,5},{2,0},{3,7},{4,6},{5,1},{6,4},{7,3},{8,10},{9,13},{10,... | collective-permute-start | bytes 4718600 | tf_op jit(solution)/shard_map/ppermute | solution.py:459
  491.3 67.5 %collective-permute-start.29 = (bf16[4,128,1024]{2,1,0:T(8,128)(2,1)S(1)}, bf16[4,128,1024]{2,1,0:T(8,128)(2,1)S(1)}, u32[]{:S(2)}, u32[]{:S(2)}) collective-permute-start(bf16[4,128,1024]{2,1,0:T(8,128)(2,1)S(1)} %dynamic-slice_bitcast_fusion), channel_id=1, source_target_pairs={{0,4},{1,3},{2,6},{3,1},{4,0},{5,7},{6,2},{7,5},{8,12},{9,11},{10,... | collective-permute-start | bytes 3145736 | tf_op jit(solution)/shard_map/ppermute | solution.py:459
  525.0 36.4 %collective-permute-start.24 = (bf16[4,32,4096]{2,1,0:T(8,128)(2,1)S(1)}, bf16[4,32,4096]{2,1,0:T(8,128)(2,1)S(1)}, u32[]{:S(2)}, u32[]{:S(2)}) collective-permute-start(bf16[4,32,4096]{2,1,0:T(8,128)(2,1)S(1)} %dynamic-slice_bitcast_fusion.5), channel_id=1, source_target_pairs={{0,4},{1,3},{2,6},{3,1},{4,0},{5,7},{6,2},{7,5},{8,12},{9,11},{10,... | collective-permute-start | bytes 3145736 | tf_op jit(solution)/shard_map/ppermute | solution.py:459
  556.2 12.6 %collective-permute-start.9 = (bf16[4,32,3072]{2,1,0:T(8,128)(2,1)S(1)}, bf16[4,32,3072]{2,1,0:T(8,128)(2,1)S(1)}, u32[]{:S(2)}, u32[]{:S(2)}) collective-permute-start(bf16[4,32,3072]{2,1,0:T(8,128)(2,1)S(1)} %dynamic-slice_bitcast_fusion.10), channel_id=1, source_target_pairs={{0,4},{1,3},{2,6},{3,1},{4,0},{5,7},{6,2},{7,5},{8,12},{9,11},{10,... | collective-permute-start | bytes 2359304 | tf_op jit(solution)/shard_map/ppermute | solution.py:459
  559.3 28.4 %collective-permute-start.30 = (bf16[2,128,1024]{2,1,0:T(8,128)(2,1)S(1)}, bf16[2,128,1024]{2,1,0:T(8,128)(2,1)S(1)}, u32[]{:S(2)}, u32[]{:S(2)}) collective-permute-start(bf16[2,128,1024]{2,1,0:T(8,128)(2,1)S(1)} %dynamic-slice_bitcast_fusion.15), channel_id=1, source_target_pairs={{0,8},{1,9},{2,10},{3,11},{4,12},{5,13},{6,14},{7,15},{8,0},{9,1},... | collective-permute-start | bytes 1572872 | tf_op jit(solution)/shard_map/ppermute | solution.py:459
  569.0 18.3 %collective-permute-start.10 = (bf16[2,32,3072]{2,1,0:T(8,128)(2,1)S(1)}, bf16[2,32,3072]{2,1,0:T(8,128)(2,1)S(1)}, u32[]{:S(2)}, u32[]{:S(2)}) collective-permute-start(bf16[2,32,3072]{2,1,0:T(8,128)(2,1)S(1)} %dynamic-slice_bitcast_fusion.17), channel_id=1, source_target_pairs={{0,8},{1,9},{2,10},{3,11},{4,12},{5,13},{6,14},{7,15},{8,0},{9,1},... | collective-permute-start | bytes 1179656 | tf_op jit(solution)/shard_map/ppermute | solution.py:459
  571.2 23.5 %collective-permute-start.25 = (bf16[2,32,4096]{2,1,0:T(8,128)(2,1)S(1)}, bf16[2,32,4096]{2,1,0:T(8,128)(2,1)S(1)}, u32[]{:S(2)}, u32[]{:S(2)}) collective-permute-start(bf16[2,32,4096]{2,1,0:T(8,128)(2,1)S(1)} %dynamic-slice_bitcast_fusion.16), channel_id=1, source_target_pairs={{0,8},{1,9},{2,10},{3,11},{4,12},{5,13},{6,14},{7,15},{8,0},{9,1},... | collective-permute-start | bytes 1572872 | tf_op jit(solution)/shard_map/ppermute | solution.py:459
  587.5 19.4 %collective-permute-start.11 = (bf16[1,32,3072]{2,1,0:T(8,128)(2,1)S(1)}, bf16[1,32,3072]{2,1,0:T(8,128)(2,1)S(1)}, u32[]{:S(2)}, u32[]{:S(2)}) collective-permute-start(bf16[1,32,3072]{2,1,0:T(8,128)(2,1)S(1)} %constant_dynamic-slice_fusion.3), channel_id=1, source_target_pairs={{0,16},{1,17},{2,18},{3,19},{4,20},{5,21},{6,22},{7,23},{8,24},{9,... | collective-permute-start | bytes 589832 | tf_op jit(solution)/shard_map/ppermute | solution.py:459
  588.0 22.0 %collective-permute-start.31 = (bf16[1,128,1024]{2,1,0:T(8,128)(2,1)S(1)}, bf16[1,128,1024]{2,1,0:T(8,128)(2,1)S(1)}, u32[]{:S(2)}, u32[]{:S(2)}) collective-permute-start(bf16[1,128,1024]{2,1,0:T(8,128)(2,1)S(1)} %constant_dynamic-slice_fusion), channel_id=1, source_target_pairs={{0,16},{1,17},{2,18},{3,19},{4,20},{5,21},{6,22},{7,23},{8,24},{9,... | collective-permute-start | bytes 786440 | tf_op jit(solution)/shard_map/ppermute | solution.py:459
  594.8 17.9 %collective-permute-start.26 = (bf16[1,32,4096]{2,1,0:T(8,128)(2,1)S(1)}, bf16[1,32,4096]{2,1,0:T(8,128)(2,1)S(1)}, u32[]{:S(2)}, u32[]{:S(2)}) collective-permute-start(bf16[1,32,4096]{2,1,0:T(8,128)(2,1)S(1)} %constant_dynamic-slice_fusion.1), channel_id=1, source_target_pairs={{0,16},{1,17},{2,18},{3,19},{4,20},{5,21},{6,22},{7,23},{8,24},{9,... | collective-permute-start | bytes 786440 | tf_op jit(solution)/shard_map/ppermute | solution.py:459
  (82 other events, 1164.1 us)
